TPU v7x, 32 devices: a whole 2x2x4 slice. The times are simulated.
32 devices in a mesh: ctx: 4 (over x, core), row: 4 (over z), col: 2 (over y).
Axes of the slice: x: 2, y: 2, z: 4, core: 2. Of those that a mesh axis runs over, the one named last changes fastest.
Arguments:
- states: bfloat16 [384, 4096], P('ctx', 'row'), may hold values from -6 to 6
- context: bfloat16 [384, 4096], P('ctx', 'row'), may hold values from -6 to 6
- up_weight: bfloat16 [4096, 8192], P('row', 'col'), may hold values from -0.09375 to 0.09375
- down_weight: bfloat16 [8192, 4096], P('col', 'row'), may hold values from -0.0625 to 0.0625
- cotangent: bfloat16 [384, 4096], P('ctx', 'row'), may hold values from -6 to 6
Outputs:
- latent: bfloat16 [384, 4096], P('ctx', 'row')
- logdet: float32 [384], P(('ctx', 'row'))
- grad_states: bfloat16 [384, 4096], P('ctx', 'row')
- grad_context: bfloat16 [384, 4096], P('ctx', 'row')
- grad_up: float32 [4096, 8192], P('row', 'col')
- grad_down: float32 [8192, 4096], P('col', 'row')
All inputs are finite; a program needn't handle non-finite values.
Results may differ from a plain program's by a relative error of at most 0.024.
Values may be sent and summed in bfloat16 or wider, within the bound.
A program may use at most 192 MiB of HBM per device.

v0:
```python
import jax
import jax.numpy as jnp
from jax import lax
from jax.sharding import PartitionSpec as P


def silu_slope(hidden):
    sigmoid_part = jax.nn.sigmoid(hidden)
    return sigmoid_part * (1.0 + hidden * (1.0 - sigmoid_part))


def collect(row_block):
    return lax.all_gather(row_block, "row", axis=0, tiled=True)


def feature_total(partial_terms):
    return lax.psum(partial_terms.astype(jnp.bfloat16), "col").astype(jnp.float32)


def contract(left_side, right_side, left_dim, right_dim):
    return lax.dot_general(
        left_side,
        right_side,
        (((left_dim,), (right_dim,)), ((), ())),
        preferred_element_type=jnp.float32,
    )


def shards(states, context, up_weight, down_weight, cotangent):
    hidden = lax.psum_scatter(
        jnp.dot(context, up_weight, preferred_element_type=jnp.float32).astype(jnp.bfloat16),
        "row",
        scatter_dimension=0,
        tiled=True,
    ).astype(jnp.float32)
    activations = collect(jax.nn.silu(hidden).astype(jnp.bfloat16))
    output_terms = jnp.dot(activations, down_weight, preferred_element_type=jnp.float32)
    mixed_total = feature_total(output_terms)
    log_scale = jnp.tanh(mixed_total)
    shrink = jnp.exp(-log_scale)
    flowed = states.astype(jnp.float32) * shrink
    cotangent_wide = cotangent.astype(jnp.float32)
    det_terms = -jnp.sum(log_scale, axis=1)
    scale_rows = ((1.0 - cotangent_wide * flowed) * (1.0 - log_scale * log_scale)).astype(
        jnp.bfloat16
    )
    down_part = contract(activations, scale_rows, 0, 0)
    grad_down = lax.psum(down_part.astype(jnp.bfloat16), "ctx").astype(jnp.float32)
    back_terms = contract(scale_rows, down_weight, 1, 1)
    back_rows = lax.psum_scatter(
        back_terms.astype(jnp.bfloat16), "row", scatter_dimension=0, tiled=True
    ).astype(jnp.float32)
    logdet = lax.psum_scatter(det_terms, "row", scatter_dimension=0, tiled=True)
    slope_rows = (back_rows * silu_slope(hidden)).astype(jnp.bfloat16)
    slope_all = collect(slope_rows)
    input_terms = contract(slope_all, up_weight, 1, 1)
    grad_states = (cotangent_wide * shrink).astype(jnp.bfloat16)
    grad_context = feature_total(input_terms).astype(jnp.bfloat16)
    up_part = contract(context, slope_all, 0, 0)
    grad_up = lax.psum(up_part.astype(jnp.bfloat16), "ctx").astype(jnp.float32)
    return (flowed.astype(jnp.bfloat16), logdet, grad_states, grad_context, grad_up, grad_down)


def solution(mesh):
    placed = (P("ctx", "row"), P("ctx", "row"), P("row", "col"), P("col", "row"), P("ctx", "row"))
    return jax.shard_map(
        shards,
        mesh=mesh,
        in_specs=placed,
        out_specs=(
            P("ctx", "row"),
            P(("ctx", "row")),
            P("ctx", "row"),
            P("ctx", "row"),
            P("row", "col"),
            P("col", "row"),
        ),
        check_vma=False,
    )
```

profile of v0, /device:TPU:0, one launch (start us, length us, event | category | flops | bytes accessed | tf_op | source)
XLA Modules:
  0.0 463.3 jit_solution(15541179772895529971)
XLA Ops:
  7.2 0.0 reduce-scatter.3.cloned.1.call-start
  7.2 0.9 copy-done
  8.1 5.7 %convolution_convert_fusion.2 = bf16[96,4096]{1,0:T(8,128)(2,1)} fusion(bf16[96,1024]{1,0:T(8,128)(2,1)S(1)} %copy-done, bf16[1024,4096]{1,0:T(8,128)(2,1)} %param.7), kind=kOutput, calls=%fused_computation.3 | convolution fusion | flops 805699584 | bytes 9371648 | tf_op jit(solution)/shard_map/dot_general | solution.py:31
  13.8 0.0 all-reduce.6.cloned.1.call-start
  13.9 26.1 %reduce-scatter.3.cloned.1.call-done = bf16[24,4096]{1,0:T(8,128)(2,1)} async-done(((bf16[96,4096]{1,0:T(8,128)(2,1)}), bf16[24,4096]{1,0:T(8,128)(2,1)}) %reduce-scatter.3.cloned.1.call-update) | async-done | bytes 196624 | tf_op jit(solution)/shard_map/reduce_scatter | solution.py:30
  40.0 1.0 fusion.7
  41.0 18.0 %all_gather.6 = bf16[96,4096]{1,0:T(8,128)(2,1)S(1)} all-gather(bf16[24,4096]{1,0:T(8,128)(2,1)S(1)} %fusion.7), channel_id=1, replica_groups=mesh['ctx'=4,'row'=4,'col'=2] {'row'}, dimensions={0}, use_global_device_ids=true | all-gather | bytes 983040 | tf_op jit(solution)/shard_map/all_gather | solution.py:13
  59.0 5.6 %convolution_convert_fusion.4 = bf16[96,1024]{1,0:T(8,128)(2,1)} fusion(bf16[96,4096]{1,0:T(8,128)(2,1)S(1)} %all_gather.6, bf16[4096,1024]{1,0:T(8,128)(2,1)} %param.8), kind=kOutput, calls=%fused_computation.5 | convolution fusion | flops 805404672 | bytes 9371648 | tf_op jit(solution)/shard_map/dot_general | solution.py:37
  64.6 0.0 all-reduce.6.cloned.1.call-update
  64.6 0.0 reduce-scatter.5.cloned.1.call-start
  64.7 21.7 %all-reduce.6.cloned.1.call-done = bf16[96,1024]{1,0:T(8,128)(2,1)} async-done(((bf16[96,1024]{1,0:T(8,128)(2,1)}), bf16[96,1024]{1,0:T(8,128)(2,1)}) %all-reduce.6.cloned.1.call-update) | async-done | bytes 196624 | tf_op jit(solution)/shard_map/psum | solution.py:17
  86.4 7.1 %convolution_convert_fusion.1 = bf16[96,4096]{1,0:T(8,128)(2,1)} fusion(bf16[4096,1024]{1,0:T(8,128)(2,1)} %param.8, bf16[96,1024]{1,0:T(8,128)(2,1)S(1)} %copy-done.2, bf16[96,1024]{1,0:T(8,128)(2,1)} %all-reduce.6.cloned.1.call-done, bf16[96,1024]{1,0:T(8,128)(2,1)S(1)} %copy-done.3), kind=kOutput, calls=%fused_computation.2 | convolution fusion | flops 806780928 | bytes 9764864 | tf_op jit(solution)/shard_map/dot_general | solution.py:21
  93.5 0.0 reduce-scatter.5.cloned.1.call-update
  93.5 0.0 all-reduce.10.cloned.1.call-start
  93.6 5.8 %convolution_convert_fusion = bf16[4096,1024]{1,0:T(8,128)(2,1)} fusion(bf16[96,4096]{1,0:T(8,128)(2,1)S(1)} %all_gather.6, bf16[96,1024]{1,0:T(8,128)(2,1)S(1)} %copy-done.2, bf16[96,1024]{1,0:T(8,128)(2,1)S(1)} %copy-done.4, bf16[96,1024]{1,0:T(8,128)(2,1)S(1)} %copy-done.3), kind=kOutput, calls=%fused_computation.1 | convolution fusion | flops 810582016 | bytes 9764864 | tf_op jit(solution)/shard_map/dot_general | solution.py:21
  99.4 17.6 %reduce-scatter.5.cloned.1.call-done = bf16[24,4096]{1,0:T(8,128)(2,1)} async-done(((bf16[96,4096]{1,0:T(8,128)(2,1)}), bf16[24,4096]{1,0:T(8,128)(2,1)}) %reduce-scatter.5.cloned.1.call-update) | async-done | bytes 196624 | tf_op jit(solution)/shard_map/reduce_scatter | solution.py:50
  117.0 1.1 fusion.11
  118.1 17.9 %all_gather.7 = bf16[96,4096]{1,0:T(8,128)(2,1)S(1)} all-gather(bf16[24,4096]{1,0:T(8,128)(2,1)S(1)} %fusion.11), channel_id=1, replica_groups=mesh['ctx'=4,'row'=4,'col'=2] {'row'}, dimensions={0}, use_global_device_ids=true | all-gather | bytes 983040 | tf_op jit(solution)/shard_map/all_gather | solution.py:13
  136.1 5.8 %convert_bitcast_fusion = bf16[1024,4096]{0,1:T(8,128)(2,1)} fusion(bf16[96,4096]{1,0:T(8,128)(2,1)S(1)} %all_gather.7, bf16[96,1024]{1,0:T(8,128)(2,1)S(1)} %copy-done), kind=kOutput, calls=%fused_computation | convolution fusion | flops 809500672 | bytes 9371648 | tf_op jit(solution)/shard_map/dot_general | solution.py:21
  141.8 0.0 all-reduce.10.cloned.1.call-update
  141.9 0.2 all-reduce.8.cloned.1.call-start
  142.1 0.4 copy-done.6
  142.5 0.6 dynamic-slice
  143.7 7.2 %convolution_convert_fusion.3 = bf16[96,1024]{1,0:T(8,128)(2,1)} fusion(bf16[96,4096]{1,0:T(8,128)(2,1)S(1)} %all_gather.7, bf16[1024,4096]{1,0:T(8,128)(2,1)} %param.7), kind=kOutput, calls=%fused_computation.4 | convolution fusion | flops 805404672 | bytes 9371648 | tf_op jit(solution)/shard_map/dot_general | solution.py:21
  151.0 1.0 fusion
  152.0 9.6 %all-reduce = f32[96]{0:T(128)S(1)} all-reduce(f32[96]{0:T(128)S(1)} %neg.13), channel_id=3, replica_groups=mesh['ctx'=4,'row'=4,'col'=2] {'row'}, use_global_device_ids=true, to_apply=%region_3.4.clone | all-reduce | flops 96 | bytes 768
  161.6 0.6 dynamic-slice.1
  162.2 268.0 %all-reduce.10.cloned.1.call-done = (bf16[1024,4096]{0,1:T(8,128)(2,1)}, bf16[4096,1024]{1,0:T(8,128)(2,1)}) async-done(((bf16[1024,4096]{0,1:T(8,128)(2,1)}, bf16[4096,1024]{1,0:T(8,128)(2,1)}), (bf16[1024,4096]{0,1:T(8,128)(2,1)}, bf16[4096,1024]{1,0:T(8,128)(2,1)})) %all-reduce.10.cloned.1.call-update) | async-done | bytes 16777232 | tf_op jit(solution)/shard_map/psum | solution.py:60
  430.1 12.3 %copy.12 = f32[1024,4096]{1,0:T(8,128)} copy(bf16[1024,4096]{0,1:T(8,128)(2,1)} %get-tuple-element.18) | data formatting | bytes 25165824
  442.5 11.8 %convert_element_type.77 = f32[4096,1024]{1,0:T(8,128)} convert(bf16[4096,1024]{1,0:T(8,128)(2,1)} %get-tuple-element.19) | non-fusion elementwise | flops 4194304 | bytes 25165824 | tf_op jit(solution)/shard_map/convert_element_type | solution.py:48
  454.2 1.0 all-reduce.8.cloned.1.call-done
  455.2 1.6 copy.17
  (15 shorter events, 0.1 us)
Async XLA Ops:
  7.2 0.9 copy-start
  7.2 32.8 %reduce-scatter.3.cloned.1.call-start = ((), (), s32[]{:S(2)}) async-start(), calls=%async_computation.2 | async-start | bytes 983040 | tf_op jit(solution)/shard_map/reduce_scatter | solution.py:30
  13.8 72.5 %all-reduce.6.cloned.1.call-start = ((), (), s32[]{:S(2)}) async-start(), calls=%async_computation.3 | async-start | bytes 393216 | tf_op jit(solution)/shard_map/psum | solution.py:17
  59.0 27.3 %copy-start.2 = (bf16[96,1024]{1,0:T(8,128)(2,1)S(1)}, bf16[96,1024]{1,0:T(8,128)(2,1)}, u32[]{:S(2)}) copy-start(bf16[96,1024]{1,0:T(8,128)(2,1)} %param.9) | copy-start | bytes 589828
  59.0 27.3 %copy-start.3 = (bf16[96,1024]{1,0:T(8,128)(2,1)S(1)}, bf16[96,1024]{1,0:T(8,128)(2,1)}, u32[]{:S(2)}) copy-start(bf16[96,1024]{1,0:T(8,128)(2,1)} %param.5) | copy-start | bytes 589828
  64.6 52.4 %reduce-scatter.5.cloned.1.call-start = ((), (), s32[]{:S(2)}) async-start(), calls=%async_computation.4 | async-start | bytes 983040 | tf_op jit(solution)/shard_map/reduce_scatter | solution.py:50
  86.4 7.2 %copy-start.4 = (bf16[96,1024]{1,0:T(8,128)(2,1)S(1)}, bf16[96,1024]{1,0:T(8,128)(2,1)}, u32[]{:S(2)}) copy-start(bf16[96,1024]{1,0:T(8,128)(2,1)} %all-reduce.6.cloned.1.call-done) | copy-start | bytes 589828
  93.5 23.5 %copy-start.5 = (bf16[24,4096]{1,0:T(8,128)(2,1)S(1)}, bf16[24,4096]{1,0:T(8,128)(2,1)}, u32[]{:S(2)}) copy-start(bf16[24,4096]{1,0:T(8,128)(2,1)} %reduce-scatter.3.cloned.1.call-done) | copy-start | bytes 589828
  93.5 336.6 %all-reduce.10.cloned.1.call-start = ((), (), s32[]{:S(2)}) async-start(), calls=%async_computation.6 | async-start | bytes 33554432 | tf_op jit(solution)/shard_map/psum | solution.py:60
  141.8 0.7 copy-start.6
  141.9 313.3 %all-reduce.8.cloned.1.call-start = ((), (), s32[]{:S(2)}) async-start(), calls=%async_computation.5 | async-start | bytes 393216 | tf_op jit(solution)/shard_map/psum | solution.py:17
  442.5 14.3 %copy-start.1 = (bf16[96,1024]{1,0:T(8,128)(2,1)S(1)}, bf16[96,1024]{1,0:T(8,128)(2,1)}, u32[]{:S(2)}) copy-start(bf16[96,1024]{1,0:T(8,128)(2,1)} %param.6) | copy-start | bytes 589828
Sparse Core Ops, SparseCore 0:
  14.0 25.9 reduce-scatter.2
  64.7 21.5 all-reduce.5
  93.6 23.3 reduce-scatter.4
  142.0 288.0 all-reduce.9
  432.8 22.3 all-reduce.7
where the time goes:
time: 464 us; the launch traced here: 463 us
  waiting for transfers between devices  334 us (72%)
  blocking collectives  45.5 us (10%)
  matrix products  37.2 us (8%)
  local copies, waits for them, and re-layouts  16.4 us (4%)
  other arithmetic  14.9 us (3%)
  between operations  14.5 us (3%)
    psum x1, waiting for transfers between devices, shards(): grad_up = lax.psum(up_part.astype(jnp.bfloat16), 'ctx').astype(jnp.float32)  268 us
    all_gather x2, blocking collectives, collect(): return lax.all_gather(row_block, 'row', axis=0, tiled=True)  35.9 us
    reduce_scatter x1, waiting for transfers between devices, shards(): lax.psum_scatter(jnp.dot(context, up_weight, preferred_element_type=jnp.f...  26.1 us
    dot_general x4, matrix products, contract(): lax.dot_general(left_side, right_side, (((left_dim,), (right_dim,)), ((),...  25.9 us
    psum x2, waiting for transfers between devices, feature_total(): lax.psum(partial_terms.astype(jnp.bfloat16), 'col').astype(jnp.float32)  22.6 us
    reduce_scatter x1, waiting for transfers between devices, shards(): lax.psum_scatter(back_terms.astype(jnp.bfloat16), 'row', scatter_dimensio...  17.6 us
    unnamed x18, local copies, waits for them, and re-layouts  16.4 us
    convert_element_type x1, other arithmetic, shards(): lax.psum(down_part.astype(jnp.bfloat16), 'ctx').astype(jnp.float32)  11.8 us
  transfers between devices with their start and end apart: 5, of which 5 were waited for; matrix products, arithmetic and copies ran while one was open for 8% of the time, Pallas kernels for 0%

commit v1 on v0

--- a/solution.py
+++ b/solution.py
@@ -11,6 +11,10 @@
 
 def collect(row_block):
     return lax.all_gather(row_block, "row", axis=0, tiled=True)
+
+
+def every_patch(group_rows):
+    return lax.all_gather(group_rows, "ctx", axis=0, tiled=True)
 
 
 def feature_total(partial_terms):
@@ -44,8 +48,7 @@
     scale_rows = ((1.0 - cotangent_wide * flowed) * (1.0 - log_scale * log_scale)).astype(
         jnp.bfloat16
     )
-    down_part = contract(activations, scale_rows, 0, 0)
-    grad_down = lax.psum(down_part.astype(jnp.bfloat16), "ctx").astype(jnp.float32)
+    grad_down = contract(every_patch(activations), every_patch(scale_rows), 0, 0)
     back_terms = contract(scale_rows, down_weight, 1, 1)
     back_rows = lax.psum_scatter(
         back_terms.astype(jnp.bfloat16), "row", scatter_dimension=0, tiled=True
@@ -56,8 +59,7 @@
     input_terms = contract(slope_all, up_weight, 1, 1)
     grad_states = (cotangent_wide * shrink).astype(jnp.bfloat16)
     grad_context = feature_total(input_terms).astype(jnp.bfloat16)
-    up_part = contract(context, slope_all, 0, 0)
-    grad_up = lax.psum(up_part.astype(jnp.bfloat16), "ctx").astype(jnp.float32)
+    grad_up = contract(every_patch(context), every_patch(slope_all), 0, 0)
     return (flowed.astype(jnp.bfloat16), logdet, grad_states, grad_context, grad_up, grad_down)
 
 

time: 464 us -> 231 us (0.50)
  waiting for transfers between devices: 334 us -> 71.3 us
  blocking collectives: 45.5 us -> 73.3 us
  other arithmetic: 14.9 us -> 4.14 us
  matrix products: 37.2 us -> 46.2 us
    psum x1 -> x0, waiting for transfers between devices: 268 us -> none  [shards(): grad_up = lax.psum(up_part.astype(jnp.bfloat16), 'ctx').astype(jnp.float32)]
    all_gather x0 -> x2, blocking collectives: none -> 25.8 us  [every_patch(): return lax.all_gather(group_rows, 'ctx', axis=0, tiled=True)]
    convert_element_type x2 -> x1, other arithmetic: 12.8 us -> 2.01 us  [shards(): ((1.0 - cotangent_wide * flowed) * (1.0 - log_scale * log_scale)).astype(...]
    dot_general x4, matrix products: 25.9 us -> 34.6 us  [contract(): lax.dot_general(left_side, right_side, (((left_dim,), (right_dim,)), ((),...]
    reduce_scatter x1, waiting for transfers between devices: 17.6 us -> 22.8 us  [shards(): lax.psum_scatter(back_terms.astype(jnp.bfloat16), 'row', scatter_dimensio...]
    unnamed x18 -> x16, local copies, waits for them, and re-layouts: 16.4 us -> 20.3 us
  transfers between devices with their start and end apart: 5 -> 6, of which waited for: 5 -> 3; matrix products, arithmetic and copies ran while one was open for 8% -> 21% of each run, Pallas kernels for 0% -> 0%
where the time goes in v1:
time: 231 us; the launch traced here: 230 us
  blocking collectives  73.3 us (32%)
  waiting for transfers between devices  71.3 us (31%)
  matrix products  46.2 us (20%)
  local copies, waits for them, and re-layouts  20.3 us (9%)
  between operations  14.8 us (6%)
  other arithmetic  4.14 us (2%)
    all_gather x2, blocking collectives, collect(): return lax.all_gather(row_block, 'row', axis=0, tiled=True)  36.4 us
    dot_general x4, matrix products, contract(): lax.dot_general(left_side, right_side, (((left_dim,), (right_dim,)), ((),...  34.6 us
    reduce_scatter x1, waiting for transfers between devices, shards(): lax.psum_scatter(jnp.dot(context, up_weight, preferred_element_type=jnp.f...  26.1 us
    all_gather x2, blocking collectives, every_patch(): return lax.all_gather(group_rows, 'ctx', axis=0, tiled=True)  25.8 us
    reduce_scatter x1, waiting for transfers between devices, shards(): lax.psum_scatter(back_terms.astype(jnp.bfloat16), 'row', scatter_dimensio...  22.8 us
    psum x2, waiting for transfers between devices, feature_total(): lax.psum(partial_terms.astype(jnp.bfloat16), 'col').astype(jnp.float32)  21.7 us
    unnamed x16, local copies, waits for them, and re-layouts  20.3 us
    unnamed x1, blocking collectives  11.1 us
  transfers between devices with their start and end apart: 6, of which 3 were waited for; matrix products, arithmetic and copies ran while one was open for 21% of the time, Pallas kernels for 0%

profile of v1, /device:TPU:0, one launch (start us, length us, event | category | flops | bytes accessed | tf_op | source)
XLA Modules:
  0.0 230.2 jit_solution(3813017824190808464)
XLA Ops:
  7.2 0.0 reduce-scatter.3.cloned.1.call-start
  7.2 5.8 %convolution_convert_fusion.1 = bf16[96,4096]{1,0:T(8,128)(2,1)} fusion(bf16[96,1024]{1,0:T(8,128)(2,1)} %param.6, bf16[1024,4096]{1,0:T(8,128)(2,1)} %param.7), kind=kOutput, calls=%fused_computation.2 | convolution fusion | flops 805699584 | bytes 9371648 | tf_op jit(solution)/shard_map/dot_general | solution.py:35
  13.0 0.0 reduce-scatter.3.cloned.1.call-update
  13.1 0.0 all-reduce.4.cloned.1.call-start
  13.1 26.1 %reduce-scatter.3.cloned.1.call-done = bf16[24,4096]{1,0:T(8,128)(2,1)} async-done(((bf16[96,4096]{1,0:T(8,128)(2,1)}), bf16[24,4096]{1,0:T(8,128)(2,1)}) %reduce-scatter.3.cloned.1.call-update) | async-done | bytes 196624 | tf_op jit(solution)/shard_map/reduce_scatter | solution.py:34
  39.2 1.0 fusion.7
  40.3 18.0 %all_gather.18 = bf16[96,4096]{1,0:T(8,128)(2,1)S(1)} all-gather(bf16[24,4096]{1,0:T(8,128)(2,1)S(1)} %fusion.7), channel_id=1, replica_groups=mesh['ctx'=4,'row'=4,'col'=2] {'row'}, dimensions={0}, use_global_device_ids=true | all-gather | bytes 983040 | tf_op jit(solution)/shard_map/all_gather | solution.py:13
  58.3 5.8 %convolution_convert_fusion.3 = bf16[96,1024]{1,0:T(8,128)(2,1)} fusion(bf16[96,4096]{1,0:T(8,128)(2,1)S(1)} %all_gather.18, bf16[4096,1024]{1,0:T(8,128)(2,1)} %param.8), kind=kOutput, calls=%fused_computation.4 | convolution fusion | flops 805404672 | bytes 9371648 | tf_op jit(solution)/shard_map/dot_general | solution.py:41
  64.1 0.0 all-reduce.4.cloned.1.call-update
  64.1 0.0 reduce-scatter.5.cloned.1.call-start
  64.2 21.7 %all-reduce.4.cloned.1.call-done = bf16[96,1024]{1,0:T(8,128)(2,1)} async-done(((bf16[96,1024]{1,0:T(8,128)(2,1)}), bf16[96,1024]{1,0:T(8,128)(2,1)}) %all-reduce.4.cloned.1.call-update) | async-done | bytes 196624 | tf_op jit(solution)/shard_map/psum | solution.py:21
  85.9 2.0 fusion.3
  87.9 6.9 %convolution_convert_fusion = bf16[96,4096]{1,0:T(8,128)(2,1)} fusion(bf16[96,1024]{1,0:T(8,128)(2,1)S(1)} %get-tuple-element.18, bf16[4096,1024]{1,0:T(8,128)(2,1)} %param.8), kind=kOutput, calls=%fused_computation.1 | convolution fusion | flops 805699584 | bytes 9371648 | tf_op jit(solution)/shard_map/dot_general | solution.py:25
  94.9 0.0 all-gather.5.cloned.1.call-start
  94.9 0.5 all-gather.5.cloned.1.call-update
  95.5 0.0 all-gather.3.cloned.1.call-start
  95.5 22.8 %reduce-scatter.5.cloned.1.call-done = bf16[24,4096]{1,0:T(8,128)(2,1)} async-done(((bf16[96,4096]{1,0:T(8,128)(2,1)}), bf16[24,4096]{1,0:T(8,128)(2,1)}) %reduce-scatter.5.cloned.1.call-update) | async-done | bytes 196624 | tf_op jit(solution)/shard_map/reduce_scatter | solution.py:53
  118.3 1.1 fusion.11
  119.4 18.4 %all_gather.19 = bf16[96,4096]{1,0:T(8,128)(2,1)} all-gather(bf16[24,4096]{1,0:T(8,128)(2,1)S(1)} %fusion.11), channel_id=1, replica_groups=mesh['ctx'=4,'row'=4,'col'=2] {'row'}, dimensions={0}, use_global_device_ids=true | all-gather | bytes 983040 | tf_op jit(solution)/shard_map/all_gather | solution.py:13
  137.8 0.0 all-gather.3.cloned.1.call-update
  137.9 0.0 all-reduce.6.cloned.1.call-start
  137.9 0.6 dynamic-slice
  139.2 12.5 %all_gather.21 = bf16[384,1024]{1,0:T(8,128)(2,1)S(1)} all-gather(bf16[96,1024]{1,0:T(8,128)(2,1)S(1)} %copy-done.1), channel_id=1, replica_groups=mesh['ctx'=4,'row'=4,'col'=2] {'ctx'}, dimensions={0}, use_global_device_ids=true | all-gather | bytes 983040 | tf_op jit(solution)/shard_map/all_gather | solution.py:17
  151.7 11.1 %all-reduce = f32[96]{0:T(128)S(1)} all-reduce(f32[96]{0:T(128)S(1)} %neg.13), channel_id=3, replica_groups=mesh['ctx'=4,'row'=4,'col'=2] {'row'}, use_global_device_ids=true, to_apply=%region_3.4.clone | all-reduce | flops 96 | bytes 768
  162.8 0.6 dynamic-slice.1
  163.4 13.3 %all_gather.23 = bf16[384,1024]{1,0:T(8,128)(2,1)S(1)} all-gather(bf16[96,1024]{1,0:T(8,128)(2,1)S(1)} %get-tuple-element.18), channel_id=1, replica_groups=mesh['ctx'=4,'row'=4,'col'=2] {'ctx'}, dimensions={0}, use_global_device_ids=true | all-gather | bytes 983040 | tf_op jit(solution)/shard_map/all_gather | solution.py:17
  176.7 7.1 %convolution_convert_fusion.2 = bf16[96,1024]{1,0:T(8,128)(2,1)} fusion(bf16[96,4096]{1,0:T(8,128)(2,1)} %all_gather.19, bf16[1024,4096]{1,0:T(8,128)(2,1)} %param.7), kind=kOutput, calls=%fused_computation.3 | convolution fusion | flops 805404672 | bytes 9371648 | tf_op jit(solution)/shard_map/dot_general | solution.py:25
  183.8 0.0 all-gather.5.cloned.1.call-done
  183.8 10.5 %fusion.15 = f32[4096,1024]{1,0:T(8,128)} fusion(bf16[384,4096]{1,0:T(8,128)(2,1)} %all-gather.5.cloned.1.call-done, bf16[384,1024]{1,0:T(8,128)(2,1)S(1)} %all_gather.23), kind=kOutput, calls=%fused_computation.27 | convolution fusion | flops 3221225472 | bytes 20709376 | tf_op jit(solution)/shard_map/dot_general | solution.py:25
  194.2 10.1 %convolution_bitcast_fusion = f32[1024,4096]{0,1:T(8,128)} fusion(bf16[384,4096]{1,0:T(8,128)(2,1)} %all-gather.3.cloned.1.call-done, bf16[384,1024]{1,0:T(8,128)(2,1)S(1)} %all_gather.21), kind=kOutput, calls=%fused_computation | convolution fusion | flops 3221225472 | bytes 20709376 | tf_op jit(solution)/shard_map/dot_general | solution.py:25
  204.3 17.5 %copy.12 = f32[1024,4096]{1,0:T(8,128)} copy(f32[1024,4096]{0,1:T(8,128)} %convolution_bitcast_fusion) | data formatting | bytes 33554432
  221.8 1.6 copy.15
  (17 shorter events, 0.1 us)
Async XLA Ops:
  7.2 32.1 %reduce-scatter.3.cloned.1.call-start = ((), (), s32[]{:S(2)}) async-start(), calls=%async_computation.2 | async-start | bytes 983040 | tf_op jit(solution)/shard_map/reduce_scatter | solution.py:34
  13.1 72.8 %all-reduce.4.cloned.1.call-start = ((), (), s32[]{:S(2)}) async-start(), calls=%async_computation.3 | async-start | bytes 393216 | tf_op jit(solution)/shard_map/psum | solution.py:21
  58.3 5.8 %copy-start = (bf16[96,4096]{1,0:T(8,128)(2,1)}, bf16[96,4096]{1,0:T(8,128)(2,1)S(1)}, u32[]{:S(2)}) copy-start(bf16[96,4096]{1,0:T(8,128)(2,1)S(1)} %all_gather.18) | copy-start | bytes 2359300
  58.3 27.6 %copy-start.3 = (bf16[96,1024]{1,0:T(8,128)(2,1)S(1)}, bf16[96,1024]{1,0:T(8,128)(2,1)}, u32[]{:S(2)}) copy-start(bf16[96,1024]{1,0:T(8,128)(2,1)} %param.9) | copy-start | bytes 589828
  58.3 27.6 %copy-start.4 = (bf16[96,1024]{1,0:T(8,128)(2,1)S(1)}, bf16[96,1024]{1,0:T(8,128)(2,1)}, u32[]{:S(2)}) copy-start(bf16[96,1024]{1,0:T(8,128)(2,1)} %param.5) | copy-start | bytes 589828
  64.1 54.2 %copy-start.2 = (bf16[24,4096]{1,0:T(8,128)(2,1)S(1)}, bf16[24,4096]{1,0:T(8,128)(2,1)}, u32[]{:S(2)}) copy-start(bf16[24,4096]{1,0:T(8,128)(2,1)} %reduce-scatter.3.cloned.1.call-done) | copy-start | bytes 589828
  64.1 73.8 %copy-start.5 = (u32[32]{0:T(128)S(1)}, u32[32]{0:T(128)}, u32[]{:S(2)}) copy-start(u32[32]{0:T(128)} %constant.9) | copy-start | bytes 388
  64.1 75.1 %copy-start.1 = (bf16[96,1024]{1,0:T(8,128)(2,1)S(1)}, bf16[96,1024]{1,0:T(8,128)(2,1)}, u32[]{:S(2)}) copy-start(bf16[96,1024]{1,0:T(8,128)(2,1)} %param.6) | copy-start | bytes 589828
  64.1 54.2 %reduce-scatter.5.cloned.1.call-start = ((), (), s32[]{:S(2)}) async-start(), calls=%async_computation.4 | async-start | bytes 983040 | tf_op jit(solution)/shard_map/reduce_scatter | solution.py:53
  94.9 88.9 %all-gather.5.cloned.1.call-start = ((), (), s32[]{:S(2)}) async-start(), calls=%async_computation.7 | async-start | bytes 3932160 | tf_op jit(solution)/shard_map/all_gather | solution.py:17
  95.5 98.8 %all-gather.3.cloned.1.call-start = ((), (), s32[]{:S(2)}) async-start(), calls=%async_computation.6 | async-start | bytes 3932160 | tf_op jit(solution)/shard_map/all_gather | solution.py:17
  137.9 83.9 %all-reduce.6.cloned.1.call-start = ((), (), s32[]{:S(2)}) async-start(), calls=%async_computation.5 | async-start | bytes 393216 | tf_op jit(solution)/shard_map/psum | solution.py:21
Sparse Core Ops, SparseCore 0:
  13.2 25.9 reduce-scatter.2
  64.3 21.5 all-reduce.3
  95.0 23.2 reduce-scatter.4
  120.3 31.6 all-gather.4
  153.5 33.0 all-gather.2
  189.2 21.8 all-reduce.5

commit v2 on v1

v2 whole, which is shorter than its diff:
```python
import functools

import jax
import jax.numpy as jnp
from jax import lax
from jax.experimental import pallas as pl
from jax.experimental.pallas import tpu as pltpu
from jax.sharding import PartitionSpec as P


def silu_slope(hidden):
    sigmoid_part = jax.nn.sigmoid(hidden)
    return sigmoid_part * (1.0 + hidden * (1.0 - sigmoid_part))


def collect(row_block):
    return lax.all_gather(row_block, "row", axis=0, tiled=True)


def every_patch(group_rows, ways):
    blocks = [group_rows]
    bit = ways // 2
    while bit:
        pairs = [(i, i ^ bit) for i in range(ways)]
        blocks = blocks + [lax.ppermute(block, "ctx", pairs) for block in blocks]
        bit //= 2
    return blocks


def feature_total(partial_terms, ways):
    sent = partial_terms.astype(jnp.bfloat16)
    if ways != 2:
        return lax.psum(sent, "col").astype(jnp.float32)
    other = lax.ppermute(sent, "col", [(0, 1), (1, 0)])
    return sent.astype(jnp.float32) + other.astype(jnp.float32)


def row_pieces(values, ways):
    me = lax.axis_index("row")
    rows = values.shape[0] // ways
    total = None
    for shift in range(1, ways):
        piece = lax.dynamic_slice_in_dim(values, (me + shift) % ways * rows, rows)
        came = lax.ppermute(piece, "row", [(i, (i + shift) % ways) for i in range(ways)])
        total = came.astype(jnp.float32) if total is None else total + came.astype(jnp.float32)
    return total + lax.dynamic_slice_in_dim(values, me * rows, rows).astype(jnp.float32)


def row_scatter(partial_terms, ways):
    sent = partial_terms.astype(jnp.bfloat16)
    if ways == 4:
        return row_pieces(sent, ways)
    return lax.psum_scatter(sent, "row", scatter_dimension=0, tiled=True).astype(jnp.float32)


def contract(left_side, right_side, left_dim, right_dim):
    return lax.dot_general(
        left_side,
        right_side,
        (((left_dim,), (right_dim,)), ((), ())),
        preferred_element_type=jnp.float32,
    )


def outer_kernel(count, *refs):
    lefts, rights, out_ref = refs[:count], refs[count : 2 * count], refs[2 * count]
    left = jnp.concatenate([ref[...] for ref in lefts], axis=0)
    right = jnp.concatenate([ref[...] for ref in rights], axis=0)
    out_ref[...] = contract(left, right, 0, 0)


def outer_total(lefts, rights):
    count = len(lefts)
    patches, height = lefts[0].shape
    width = rights[0].shape[1]
    tall = height >= width
    tile = min(512, max(height, width))
    if tall:
        left_spec = pl.BlockSpec((patches, tile), lambda i: (0, i))
        right_spec = pl.BlockSpec((patches, width), lambda i: (0, 0))
        out_spec = pl.BlockSpec((tile, width), lambda i: (i, 0))
    else:
        left_spec = pl.BlockSpec((patches, height), lambda i: (0, 0))
        right_spec = pl.BlockSpec((patches, tile), lambda i: (0, i))
        out_spec = pl.BlockSpec((height, tile), lambda i: (0, i))
    return pl.pallas_call(
        functools.partial(outer_kernel, count),
        grid=(max(height, width) // tile,),
        in_specs=[left_spec] * count + [right_spec] * count,
        out_specs=out_spec,
        out_shape=jax.ShapeDtypeStruct((height, width), jnp.float32),
        compiler_params=pltpu.CompilerParams(vmem_limit_bytes=40 * 1024 * 1024),
        cost_estimate=pl.CostEstimate(
            flops=2 * count * patches * height * width,
            bytes_accessed=4 * height * width + 2 * count * patches * (height + width),
            transcendentals=0,
        ),
    )(*lefts, *rights)


def shards(n_ctx, n_row, n_col, states, context, up_weight, down_weight, cotangent):
    hidden = row_scatter(jnp.dot(context, up_weight, preferred_element_type=jnp.float32), n_row)
    context_blocks = every_patch(context, n_ctx)
    activations = collect(jax.nn.silu(hidden).astype(jnp.bfloat16))
    acts_blocks = every_patch(activations, n_ctx)
    output_terms = jnp.dot(activations, down_weight, preferred_element_type=jnp.float32)
    log_scale = jnp.tanh(feature_total(output_terms, n_col))
    shrink = jnp.exp(-log_scale)
    flowed = states.astype(jnp.float32) * shrink
    cotangent_wide = cotangent.astype(jnp.float32)
    det_terms = -jnp.sum(log_scale, axis=1)
    scale_rows = ((1.0 - cotangent_wide * flowed) * (1.0 - log_scale * log_scale)).astype(
        jnp.bfloat16
    )
    back_terms = contract(scale_rows, down_weight, 1, 1)
    back_rows = row_scatter(back_terms, n_row)
    scale_blocks = every_patch(scale_rows, n_ctx)
    grad_down = outer_total(acts_blocks, scale_blocks)
    if n_row == 4:
        logdet = row_pieces(det_terms, n_row)
    else:
        logdet = lax.psum_scatter(det_terms, "row", scatter_dimension=0, tiled=True)
    slope_rows = (back_rows * silu_slope(hidden)).astype(jnp.bfloat16)
    slope_all = collect(slope_rows)
    slope_blocks = every_patch(slope_all, n_ctx)
    input_terms = contract(slope_all, up_weight, 1, 1)
    grad_states = (cotangent_wide * shrink).astype(jnp.bfloat16)
    grad_context = feature_total(input_terms, n_col).astype(jnp.bfloat16)
    grad_up = outer_total(context_blocks, slope_blocks)
    return (flowed.astype(jnp.bfloat16), logdet, grad_states, grad_context, grad_up, grad_down)


def solution(mesh):
    placed = (P("ctx", "row"), P("ctx", "row"), P("row", "col"), P("col", "row"), P("ctx", "row"))
    return jax.shard_map(
        functools.partial(shards, mesh.shape["ctx"], mesh.shape["row"], mesh.shape["col"]),
        mesh=mesh,
        in_specs=placed,
        out_specs=(
            P("ctx", "row"),
            P(("ctx", "row")),
            P("ctx", "row"),
            P("ctx", "row"),
            P("row", "col"),
            P("col", "row"),
        ),
        check_vma=False,
    )
```

time: 231 us -> 150 us (0.65)
  blocking collectives: 73.3 us -> 40 us
  matrix products: 46.2 us -> 15.3 us
  starting transfers between devices: 0.24 us -> 24.8 us
  waiting for transfers between devices: 71.3 us -> 47.3 us
  local copies, waits for them, and re-layouts: 20.3 us -> 0.22 us
  Pallas kernels: 0 us -> 18.3 us
  between operations: 14.8 us -> 0.84 us
    reduce_scatter x2 -> x0, waiting for transfers between devices: 48.9 us -> none  [the longest x1 26.1 us: shards(): lax.psum_scatter(jnp.dot(context, up_weight, preferred_element_type=jnp.f...]
    ppermute x0 -> x23, waiting for transfers between devices: none -> 47.3 us  [the longest x9 21.1 us: row_pieces(): lax.ppermute(piece, 'row', [(i, (i + shift) % ways) for i in range(ways)])]
    dot_general x4 -> x2, matrix products: 34.6 us -> 5.37 us  [contract(): lax.dot_general(left_side, right_side, (((left_dim,), (right_dim,)), ((),...]
    all_gather x2 -> x0, blocking collectives: 25.8 us -> none  [every_patch(): return lax.all_gather(group_rows, 'ctx', axis=0, tiled=True)]
    ppermute x0 -> x23, starting transfers between devices: none -> 24.8 us  [the longest x9 15.1 us: row_pieces(): lax.ppermute(piece, 'row', [(i, (i + shift) % ways) for i in range(ways)])]
    psum x2 -> x0, waiting for transfers between devices: 21.7 us -> none  [feature_total(): lax.psum(partial_terms.astype(jnp.bfloat16), 'col').astype(jnp.float32)]
    unnamed x16 -> x14, local copies, waits for them, and re-layouts: 20.3 us -> 0.04 us
    pallas_call x0 -> x2, Pallas kernels: none -> 18.3 us  [outer_total(): pl.pallas_call(functools.partial(outer_kernel, count), grid=(max(height,...]
  transfers between devices with their start and end apart: 6 -> 23, of which waited for: 3 -> 10; matrix products, arithmetic and copies ran while one was open for 21% -> 3% of each run, Pallas kernels for 0% -> 6%
where the time goes in v2:
time: 150 us
  waiting for transfers between devices  47.3 us (32%)
  blocking collectives  40 us (27%)
  starting transfers between devices  24.8 us (17%)
  Pallas kernels  18.3 us (12%)
  matrix products  15.3 us (10%)
  other arithmetic  2.89 us (2%)
    all_gather x2, blocking collectives, collect(): return lax.all_gather(row_block, 'row', axis=0, tiled=True)  40 us
    ppermute x9, waiting for transfers between devices, row_pieces(): lax.ppermute(piece, 'row', [(i, (i + shift) % ways) for i in range(ways)])  21.1 us
    pallas_call x2, Pallas kernels, outer_total(): pl.pallas_call(functools.partial(outer_kernel, count), grid=(max(height,...  18.3 us
    ppermute x12, waiting for transfers between devices, every_patch(): blocks = blocks + [lax.ppermute(block, 'ctx', pairs) for block in blocks]  17.2 us
    ppermute x9, starting transfers between devices, row_pieces(): lax.ppermute(piece, 'row', [(i, (i + shift) % ways) for i in range(ways)])  15.1 us
    ppermute x2, waiting for transfers between devices, feature_total(): other = lax.ppermute(sent, 'col', [(0, 1), (1, 0)])  8.93 us
    ppermute x12, starting transfers between devices, every_patch(): blocks = blocks + [lax.ppermute(block, 'ctx', pairs) for block in blocks]  6.54 us
    dot_general x2, matrix products, contract(): lax.dot_general(left_side, right_side, (((left_dim,), (right_dim,)), ((),...  5.37 us
  transfers between devices with their start and end apart: 23, of which 10 were waited for; matrix products, arithmetic and copies ran while one was open for 3% of the time, Pallas kernels for 6%

profile of v2, /device:TPU:0, one launch (start us, length us, event | category | flops | bytes accessed | tf_op | source)
XLA Modules:
  0.0 149.6 jit_solution(9262451833958923900)
XLA Ops:
  0.7 5.0 %convolution_convert_fusion.1 = bf16[96,4096]{1,0:T(8,128)(2,1)S(1)} fusion(bf16[96,1024]{1,0:T(8,128)(2,1)} %refs_0_.1, bf16[1024,4096]{1,0:T(8,128)(2,1)} %param.7), kind=kOutput, calls=%fused_computation.1 | convolution fusion | flops 805699584 | bytes 9371648 | tf_op jit(solution)/shard_map/dot_general | solution.py:102
  5.7 3.1 %collective-permute-start = (bf16[24,4096]{1,0:T(8,128)(2,1)S(1)}, bf16[24,4096]{1,0:T(8,128)(2,1)S(1)}, u32[]{:S(2)}, u32[]{:S(2)}) collective-permute-start(bf16[24,4096]{1,0:T(8,128)(2,1)S(1)} %get-tuple-element.9), channel_id=1, source_target_pairs={{0,2},{2,4},{4,6},{6,0},{1,3},{3,5},{5,7},{7,1},{8,10},{10,12},{12... | collective-permute-start | bytes 589832 | tf_op jit(solution)/shard_map/ppermute | solution.py:44
  8.8 2.6 %collective-permute-start.1 = (bf16[24,4096]{1,0:T(8,128)(2,1)S(1)}, bf16[24,4096]{1,0:T(8,128)(2,1)S(1)}, u32[]{:S(2)}, u32[]{:S(2)}) collective-permute-start(bf16[24,4096]{1,0:T(8,128)(2,1)S(1)} %get-tuple-element.11), channel_id=1, source_target_pairs={{0,4},{2,6},{4,0},{6,2},{1,5},{3,7},{5,1},{7,3},{8,12},{10,14},{12... | collective-permute-start | bytes 589832 | tf_op jit(solution)/shard_map/ppermute | solution.py:44
  11.4 1.3 collective-permute-start.2
  12.7 3.9 %collective-permute-done = bf16[24,4096]{1,0:T(8,128)(2,1)S(1)} collective-permute-done((bf16[24,4096]{1,0:T(8,128)(2,1)S(1)}, bf16[24,4096]{1,0:T(8,128)(2,1)S(1)}, u32[]{:S(2)}, u32[]{:S(2)}) %collective-permute-start) | collective-permute-done | bytes 196640 | tf_op jit(solution)/shard_map/ppermute | solution.py:44
  16.7 7.6 %collective-permute-done.1 = bf16[24,4096]{1,0:T(8,128)(2,1)S(1)} collective-permute-done((bf16[24,4096]{1,0:T(8,128)(2,1)S(1)}, bf16[24,4096]{1,0:T(8,128)(2,1)S(1)}, u32[]{:S(2)}, u32[]{:S(2)}) %collective-permute-start.1) | collective-permute-done | bytes 196640 | tf_op jit(solution)/shard_map/ppermute | solution.py:44
  24.4 22.2 %all_gather.6.refs_0_ = bf16[96,4096]{1,0:T(8,128)(2,1)S(1)} all-gather(bf16[24,4096]{1,0:T(8,128)(2,1)S(1)} %multiply_convert_fusion.1), channel_id=1, replica_groups=mesh['ctx'=4,'row'=4,'col'=2] {'row'}, dimensions={0}, use_global_device_ids=true | all-gather | bytes 983040 | tf_op jit(solution)/shard_map/all_gather | solution.py:17
  46.7 5.0 %convolution_convert_fusion.3 = bf16[96,1024]{1,0:T(8,128)(2,1)S(1)} fusion(bf16[96,4096]{1,0:T(8,128)(2,1)S(1)} %all_gather.6.refs_0_, bf16[4096,1024]{1,0:T(8,128)(2,1)} %param.8), kind=kOutput, calls=%fused_computation.3 | convolution fusion | flops 805404672 | bytes 9371648 | tf_op jit(solution)/shard_map/dot_general | solution.py:106
  51.7 1.6 %collective-permute-start.3 = (bf16[96,1024]{1,0:T(8,128)(2,1)S(1)}, bf16[96,1024]{1,0:T(8,128)(2,1)S(1)}, u32[]{:S(2)}, u32[]{:S(2)}) collective-permute-start(bf16[96,1024]{1,0:T(8,128)(2,1)S(1)} %convolution_convert_fusion.3), channel_id=1, source_target_pairs={{0,1},{1,0},{2,3},{3,2},{4,5},{5,4},{6,7},{7,6},{8,9},{9,8},{10,11... | collective-permute-start | bytes 589832 | tf_op jit(solution)/shard_map/ppermute | solution.py:34
  53.2 4.2 %collective-permute-done.3 = bf16[96,1024]{1,0:T(8,128)(2,1)S(1)} collective-permute-done((bf16[96,1024]{1,0:T(8,128)(2,1)S(1)}, bf16[96,1024]{1,0:T(8,128)(2,1)S(1)}, u32[]{:S(2)}, u32[]{:S(2)}) %collective-permute-start.3) | collective-permute-done | bytes 196640 | tf_op jit(solution)/shard_map/ppermute | solution.py:34
  57.4 1.1 fusion.3
  58.5 2.7 %convolution_convert_fusion = bf16[96,4096]{1,0:T(8,128)(2,1)S(1)} fusion(bf16[96,1024]{1,0:T(8,128)(2,1)S(1)} %get-tuple-element.12.refs_4_, bf16[4096,1024]{1,0:T(8,128)(2,1)S(1)} %bitcast.9), kind=kOutput, calls=%fused_computation | convolution fusion | flops 805699584 | bytes 9371648 | tf_op jit(solution)/shard_map/dot_general | solution.py:57
  61.3 2.2 %collective-permute-start.8 = (bf16[24,4096]{1,0:T(8,128)(2,1)S(1)}, bf16[24,4096]{1,0:T(8,128)(2,1)S(1)}, u32[]{:S(2)}, u32[]{:S(2)}) collective-permute-start(bf16[24,4096]{1,0:T(8,128)(2,1)S(1)} %get-tuple-element.8), channel_id=1, source_target_pairs={{0,4},{2,6},{4,0},{6,2},{1,5},{3,7},{5,1},{7,3},{8,12},{10,14},{12... | collective-permute-start | bytes 589832 | tf_op jit(solution)/shard_map/ppermute | solution.py:44
  63.5 1.6 %collective-permute-start.9 = (bf16[24,4096]{1,0:T(8,128)(2,1)S(1)}, bf16[24,4096]{1,0:T(8,128)(2,1)S(1)}, u32[]{:S(2)}, u32[]{:S(2)}) collective-permute-start(bf16[24,4096]{1,0:T(8,128)(2,1)S(1)} %get-tuple-element.7), channel_id=1, source_target_pairs={{0,6},{2,0},{4,2},{6,4},{1,7},{3,1},{5,3},{7,5},{8,14},{10,8},{12,... | collective-permute-start | bytes 589832 | tf_op jit(solution)/shard_map/ppermute | solution.py:44
  65.1 1.5 collective-permute-start.17
  66.6 2.4 %collective-permute-done.7 = bf16[24,4096]{1,0:T(8,128)(2,1)S(1)} collective-permute-done((bf16[24,4096]{1,0:T(8,128)(2,1)S(1)}, bf16[24,4096]{1,0:T(8,128)(2,1)S(1)}, u32[]{:S(2)}, u32[]{:S(2)}) %collective-permute-start.7) | collective-permute-done | bytes 196640 | tf_op jit(solution)/shard_map/ppermute | solution.py:44
  69.0 5.3 %collective-permute-done.8 = bf16[24,4096]{1,0:T(8,128)(2,1)S(1)} collective-permute-done((bf16[24,4096]{1,0:T(8,128)(2,1)S(1)}, bf16[24,4096]{1,0:T(8,128)(2,1)S(1)}, u32[]{:S(2)}, u32[]{:S(2)}) %collective-permute-start.8) | collective-permute-done | bytes 196640 | tf_op jit(solution)/shard_map/ppermute | solution.py:44
  74.6 17.8 %all_gather.7.refs_4_ = bf16[96,4096]{1,0:T(8,128)(2,1)S(1)} all-gather(bf16[24,4096]{1,0:T(8,128)(2,1)S(1)} %multiply_convert_fusion), channel_id=1, replica_groups=mesh['ctx'=4,'row'=4,'col'=2] {'row'}, dimensions={0}, use_global_device_ids=true | all-gather | bytes 983040 | tf_op jit(solution)/shard_map/all_gather | solution.py:17
  92.4 1.5 collective-permute-start.14
  94.4 1.5 collective-permute-start.20
  96.2 16.5 %collective-permute-done.11.refs_1_ = bf16[96,1024]{1,0:T(8,128)(2,1)S(1)} collective-permute-done((bf16[96,1024]{1,0:T(8,128)(2,1)S(1)}, bf16[96,1024]{1,0:T(8,128)(2,1)S(1)}, u32[]{:S(2)}, u32[]{:S(2)}) %collective-permute-start.11) | collective-permute-done | bytes 196640 | tf_op jit(solution)/shard_map/ppermute | solution.py:25
  112.7 1.7 %collective-permute-start.5 = (f32[24]{0:T(128)S(1)}, f32[24]{0:T(128)S(1)}, u32[]{:S(2)}, u32[]{:S(2)}) collective-permute-start(f32[24]{0:T(128)S(1)} %get-tuple-element.16), channel_id=1, source_target_pairs={{0,4},{2,6},{4,0},{6,2},{1,5},{3,7},{5,1},{7,3},{8,12},{10,14},{12... | collective-permute-start | bytes 296 | tf_op jit(solution)/shard_map/ppermute | solution.py:44
  114.5 2.2 %collective-permute-start.6 = (f32[24]{0:T(128)S(1)}, f32[24]{0:T(128)S(1)}, u32[]{:S(2)}, u32[]{:S(2)}) collective-permute-start(f32[24]{0:T(128)S(1)} %get-tuple-element.17), channel_id=1, source_target_pairs={{0,6},{2,0},{4,2},{6,4},{1,7},{3,1},{5,3},{7,5},{8,14},{10,8},{12,... | collective-permute-start | bytes 296 | tf_op jit(solution)/shard_map/ppermute | solution.py:44
  117.2 1.4 collective-permute-done.6
  119.6 2.7 %convolution_convert_fusion.2 = bf16[96,1024]{1,0:T(8,128)(2,1)S(1)} fusion(bf16[96,4096]{1,0:T(8,128)(2,1)S(1)} %all_gather.7.refs_4_, bf16[1024,4096]{1,0:T(8,128)(2,1)S(1)} %bitcast.11), kind=kOutput, calls=%fused_computation.2 | convolution fusion | flops 805404672 | bytes 9371648 | tf_op jit(solution)/shard_map/dot_general | solution.py:57
  122.3 1.6 %collective-permute-start.10 = (bf16[96,1024]{1,0:T(8,128)(2,1)S(1)}, bf16[96,1024]{1,0:T(8,128)(2,1)S(1)}, u32[]{:S(2)}, u32[]{:S(2)}) collective-permute-start(bf16[96,1024]{1,0:T(8,128)(2,1)S(1)} %convolution_convert_fusion.2), channel_id=1, source_target_pairs={{0,1},{1,0},{2,3},{3,2},{4,5},{5,4},{6,7},{7,6},{8,9},{9,8},{10,11... | collective-permute-start | bytes 589832 | tf_op jit(solution)/shard_map/ppermute | solution.py:34
  123.9 0.6 dynamic-slice_add_fusion
  124.5 4.8 %collective-permute-done.10 = bf16[96,1024]{1,0:T(8,128)(2,1)S(1)} collective-permute-done((bf16[96,1024]{1,0:T(8,128)(2,1)S(1)}, bf16[96,1024]{1,0:T(8,128)(2,1)S(1)}, u32[]{:S(2)}, u32[]{:S(2)}) %collective-permute-start.10) | collective-permute-done | bytes 196640 | tf_op jit(solution)/shard_map/ppermute | solution.py:34
  129.3 0.7 add_convert_fusion
  130.0 0.7 collective-permute-done.22.refs_7_
  131.2 9.2 %shard_map.101 = f32[4096,1024]{1,0:T(8,128)} custom-call(bf16[96,4096]{1,0:T(8,128)(2,1)S(1)} %all_gather.6.refs_0_, bf16[96,4096]{1,0:T(8,128)(2,1)S(1)} %collective-permute-done.17.refs_1_, bf16[96,4096]{1,0:T(8,128)(2,1)S(1)} %collective-permute-done.18.refs_2_, bf16[96,4096]{1,0:T(8,128)(2,1)S(1)} %collective-permute-done.19.refs_3_, ...), custom_call_target="tpu_custom_call" | custom-call | flops 3221225472 | bytes 20709376 | tf_op jit(solution)/shard_map/pallas_call | solution.py:86
  140.4 9.2 %shard_map.100 = f32[1024,4096]{1,0:T(8,128)} custom-call(bf16[96,1024]{1,0:T(8,128)(2,1)S(1)} %copy-done, bf16[96,1024]{1,0:T(8,128)(2,1)S(1)} %collective-permute-done.11.refs_1_, bf16[96,1024]{1,0:T(8,128)(2,1)S(1)} %collective-permute-done.12.refs_2_, bf16[96,1024]{1,0:T(8,128)(2,1)S(1)} %collective-permute-done.13.refs_3_, ...), custom_call_target="tpu_custom_call" | custom-call | flops 3221225472 | bytes 20709376 | tf_op jit(solution)/shard_map/pallas_call | solution.py:86
  (47 shorter events, 3.6 us)
Async XLA Ops:
  5.7 11.0 %collective-permute-start = (bf16[24,4096]{1,0:T(8,128)(2,1)S(1)}, bf16[24,4096]{1,0:T(8,128)(2,1)S(1)}, u32[]{:S(2)}, u32[]{:S(2)}) collective-permute-start(bf16[24,4096]{1,0:T(8,128)(2,1)S(1)} %get-tuple-element.9), channel_id=1, source_target_pairs={{0,2},{2,4},{4,6},{6,0},{1,3},{3,5},{5,7},{7,1},{8,10},{10,12},{12... | collective-permute-start | bytes 589832 | tf_op jit(solution)/shard_map/ppermute | solution.py:44
  8.8 15.5 %collective-permute-start.1 = (bf16[24,4096]{1,0:T(8,128)(2,1)S(1)}, bf16[24,4096]{1,0:T(8,128)(2,1)S(1)}, u32[]{:S(2)}, u32[]{:S(2)}) collective-permute-start(bf16[24,4096]{1,0:T(8,128)(2,1)S(1)} %get-tuple-element.11), channel_id=1, source_target_pairs={{0,4},{2,6},{4,0},{6,2},{1,5},{3,7},{5,1},{7,3},{8,12},{10,14},{12... | collective-permute-start | bytes 589832 | tf_op jit(solution)/shard_map/ppermute | solution.py:44
  11.4 12.9 %collective-permute-start.2 = (bf16[24,4096]{1,0:T(8,128)(2,1)S(1)}, bf16[24,4096]{1,0:T(8,128)(2,1)S(1)}, u32[]{:S(2)}, u32[]{:S(2)}) collective-permute-start(bf16[24,4096]{1,0:T(8,128)(2,1)S(1)} %get-tuple-element.10), channel_id=1, source_target_pairs={{0,6},{2,0},{4,2},{6,4},{1,7},{3,1},{5,3},{7,5},{8,14},{10,8},{12,... | collective-permute-start | bytes 589832 | tf_op jit(solution)/shard_map/ppermute | solution.py:44
  24.4 34.1 %slice-start = ((s8[8388608]{0:T(1024)(128)(4,1)}), s8[4194304]{0:T(1024)(128)(4,1)S(1)}, s32[]{:S(2)}) async-start(s8[8388608]{0:T(1024)(128)(4,1)} %bitcast.8), calls=%async_computation | async-start | bytes 8388608
  24.4 95.2 %slice-start.2 = ((s8[8388608]{0:T(1024)(128)(4,1)}), s8[4194304]{0:T(1024)(128)(4,1)S(1)}, s32[]{:S(2)}) async-start(s8[8388608]{0:T(1024)(128)(4,1)} %bitcast.10), calls=%async_computation.2 | async-start | bytes 8388608
  46.6 10.8 %copy-start.1 = (bf16[96,1024]{1,0:T(8,128)(2,1)S(1)}, bf16[96,1024]{1,0:T(8,128)(2,1)}, u32[]{:S(2)}) copy-start(bf16[96,1024]{1,0:T(8,128)(2,1)} %param.9) | copy-start | bytes 589828
  46.6 10.8 %copy-start.2 = (bf16[96,1024]{1,0:T(8,128)(2,1)S(1)}, bf16[96,1024]{1,0:T(8,128)(2,1)}, u32[]{:S(2)}) copy-start(bf16[96,1024]{1,0:T(8,128)(2,1)} %param.5) | copy-start | bytes 589828
  46.6 11.9 %slice-start.1 = ((s8[8388608]{0:T(1024)(128)(4,1)}), s8[4194304]{0:T(1024)(128)(4,1)S(1)}, s32[]{:S(2)}) async-start(s8[8388608]{0:T(1024)(128)(4,1)} %bitcast.8), calls=%async_computation.1 | async-start | bytes 8388608
  46.6 73.0 %slice-start.3 = ((s8[8388608]{0:T(1024)(128)(4,1)}), s8[4194304]{0:T(1024)(128)(4,1)S(1)}, s32[]{:S(2)}) async-start(s8[8388608]{0:T(1024)(128)(4,1)} %bitcast.10), calls=%async_computation.3 | async-start | bytes 8388608
  51.6 42.3 %copy-start = (bf16[96,1024]{1,0:T(8,128)(2,1)S(1)}, bf16[96,1024]{1,0:T(8,128)(2,1)}, u32[]{:S(2)}) copy-start(bf16[96,1024]{1,0:T(8,128)(2,1)} %refs_0_.1) | copy-start | bytes 589828
  51.7 5.7 %collective-permute-start.3 = (bf16[96,1024]{1,0:T(8,128)(2,1)S(1)}, bf16[96,1024]{1,0:T(8,128)(2,1)S(1)}, u32[]{:S(2)}, u32[]{:S(2)}) collective-permute-start(bf16[96,1024]{1,0:T(8,128)(2,1)S(1)} %convolution_convert_fusion.3), channel_id=1, source_target_pairs={{0,1},{1,0},{2,3},{3,2},{4,5},{5,4},{6,7},{7,6},{8,9},{9,8},{10,11... | collective-permute-start | bytes 589832 | tf_op jit(solution)/shard_map/ppermute | solution.py:34
  61.3 7.7 %collective-permute-start.7 = (bf16[24,4096]{1,0:T(8,128)(2,1)S(1)}, bf16[24,4096]{1,0:T(8,128)(2,1)S(1)}, u32[]{:S(2)}, u32[]{:S(2)}) collective-permute-start(bf16[24,4096]{1,0:T(8,128)(2,1)S(1)} %get-tuple-element.6), channel_id=1, source_target_pairs={{0,2},{2,4},{4,6},{6,0},{1,3},{3,5},{5,7},{7,1},{8,10},{10,12},{12... | collective-permute-start | bytes 589832 | tf_op jit(solution)/shard_map/ppermute | solution.py:44
  61.3 13.0 %collective-permute-start.8 = (bf16[24,4096]{1,0:T(8,128)(2,1)S(1)}, bf16[24,4096]{1,0:T(8,128)(2,1)S(1)}, u32[]{:S(2)}, u32[]{:S(2)}) collective-permute-start(bf16[24,4096]{1,0:T(8,128)(2,1)S(1)} %get-tuple-element.8), channel_id=1, source_target_pairs={{0,4},{2,6},{4,0},{6,2},{1,5},{3,7},{5,1},{7,3},{8,12},{10,14},{12... | collective-permute-start | bytes 589832 | tf_op jit(solution)/shard_map/ppermute | solution.py:44
  63.5 10.8 %collective-permute-start.9 = (bf16[24,4096]{1,0:T(8,128)(2,1)S(1)}, bf16[24,4096]{1,0:T(8,128)(2,1)S(1)}, u32[]{:S(2)}, u32[]{:S(2)}) collective-permute-start(bf16[24,4096]{1,0:T(8,128)(2,1)S(1)} %get-tuple-element.7), channel_id=1, source_target_pairs={{0,6},{2,0},{4,2},{6,4},{1,7},{3,1},{5,3},{7,5},{8,14},{10,8},{12,... | collective-permute-start | bytes 589832 | tf_op jit(solution)/shard_map/ppermute | solution.py:44
  65.1 54.0 %collective-permute-start.17 = (bf16[96,4096]{1,0:T(8,128)(2,1)S(1)}, bf16[96,4096]{1,0:T(8,128)(2,1)S(1)}, u32[]{:S(2)}, u32[]{:S(2)}) collective-permute-start(bf16[96,4096]{1,0:T(8,128)(2,1)S(1)} %all_gather.6.refs_0_), channel_id=1, source_target_pairs={{0,16},{8,24},{16,0},{24,8},{1,17},{9,25},{17,1},{25,9},{2,18},{10... | collective-permute-start | bytes 2359304 | tf_op jit(solution)/shard_map/ppermute | solution.py:25
  92.4 26.8 %collective-permute-start.14 = (bf16[96,4096]{1,0:T(8,128)(2,1)S(1)}, bf16[96,4096]{1,0:T(8,128)(2,1)S(1)}, u32[]{:S(2)}, u32[]{:S(2)}) collective-permute-start(bf16[96,4096]{1,0:T(8,128)(2,1)S(1)} %all_gather.7.refs_4_), channel_id=1, source_target_pairs={{0,16},{8,24},{16,0},{24,8},{1,17},{9,25},{17,1},{25,9},{2,18},{10... | collective-permute-start | bytes 2359304 | tf_op jit(solution)/shard_map/ppermute | solution.py:25
  93.9 18.8 %collective-permute-start.11 = (bf16[96,1024]{1,0:T(8,128)(2,1)S(1)}, bf16[96,1024]{1,0:T(8,128)(2,1)S(1)}, u32[]{:S(2)}, u32[]{:S(2)}) collective-permute-start(bf16[96,1024]{1,0:T(8,128)(2,1)S(1)} %copy-done), channel_id=1, source_target_pairs={{0,16},{8,24},{16,0},{24,8},{1,17},{9,25},{17,1},{25,9},{2,18},{10... | collective-permute-start | bytes 589832 | tf_op jit(solution)/shard_map/ppermute | solution.py:25
  94.4 24.1 %collective-permute-start.20 = (bf16[96,1024]{1,0:T(8,128)(2,1)S(1)}, bf16[96,1024]{1,0:T(8,128)(2,1)S(1)}, u32[]{:S(2)}, u32[]{:S(2)}) collective-permute-start(bf16[96,1024]{1,0:T(8,128)(2,1)S(1)} %get-tuple-element.12.refs_4_), channel_id=1, source_target_pairs={{0,16},{8,24},{16,0},{24,8},{1,17},{9,25},{17,1},{25,9},{2,18},{10... | collective-permute-start | bytes 589832 | tf_op jit(solution)/shard_map/ppermute | solution.py:25
  96.0 18.4 %collective-permute-start.4 = (f32[24]{0:T(128)S(1)}, f32[24]{0:T(128)S(1)}, u32[]{:S(2)}, u32[]{:S(2)}) collective-permute-start(f32[24]{0:T(128)S(1)} %get-tuple-element.18), channel_id=1, source_target_pairs={{0,2},{2,4},{4,6},{6,0},{1,3},{3,5},{5,7},{7,1},{8,10},{10,12},{12... | collective-permute-start | bytes 296 | tf_op jit(solution)/shard_map/ppermute | solution.py:44
  112.7 4.4 %collective-permute-start.5 = (f32[24]{0:T(128)S(1)}, f32[24]{0:T(128)S(1)}, u32[]{:S(2)}, u32[]{:S(2)}) collective-permute-start(f32[24]{0:T(128)S(1)} %get-tuple-element.16), channel_id=1, source_target_pairs={{0,4},{2,6},{4,0},{6,2},{1,5},{3,7},{5,1},{7,3},{8,12},{10,14},{12... | collective-permute-start | bytes 296 | tf_op jit(solution)/shard_map/ppermute | solution.py:44
  114.5 4.1 %collective-permute-start.6 = (f32[24]{0:T(128)S(1)}, f32[24]{0:T(128)S(1)}, u32[]{:S(2)}, u32[]{:S(2)}) collective-permute-start(f32[24]{0:T(128)S(1)} %get-tuple-element.17), channel_id=1, source_target_pairs={{0,6},{2,0},{4,2},{6,4},{1,7},{3,1},{5,3},{7,5},{8,14},{10,8},{12,... | collective-permute-start | bytes 296 | tf_op jit(solution)/shard_map/ppermute | solution.py:44
  117.2 13.7 %collective-permute-start.18 = (bf16[96,4096]{1,0:T(8,128)(2,1)S(1)}, bf16[96,4096]{1,0:T(8,128)(2,1)S(1)}, u32[]{:S(2)}, u32[]{:S(2)}) collective-permute-start(bf16[96,4096]{1,0:T(8,128)(2,1)S(1)} %all_gather.6.refs_0_), channel_id=1, source_target_pairs={{0,8},{8,0},{16,24},{24,16},{1,9},{9,1},{17,25},{25,17},{2,10},{10... | collective-permute-start | bytes 2359304 | tf_op jit(solution)/shard_map/ppermute | solution.py:25
  118.6 3.8 %collective-permute-start.21 = (bf16[96,1024]{1,0:T(8,128)(2,1)S(1)}, bf16[96,1024]{1,0:T(8,128)(2,1)S(1)}, u32[]{:S(2)}, u32[]{:S(2)}) collective-permute-start(bf16[96,1024]{1,0:T(8,128)(2,1)S(1)} %get-tuple-element.12.refs_4_), channel_id=1, source_target_pairs={{0,8},{8,0},{16,24},{24,16},{1,9},{9,1},{17,25},{25,17},{2,10},{10... | collective-permute-start | bytes 589832 | tf_op jit(solution)/shard_map/ppermute | solution.py:25
  118.6 21.8 %collective-permute-start.15 = (bf16[96,4096]{1,0:T(8,128)(2,1)S(1)}, bf16[96,4096]{1,0:T(8,128)(2,1)S(1)}, u32[]{:S(2)}, u32[]{:S(2)}) collective-permute-start(bf16[96,4096]{1,0:T(8,128)(2,1)S(1)} %all_gather.7.refs_4_), channel_id=1, source_target_pairs={{0,8},{8,0},{16,24},{24,16},{1,9},{9,1},{17,25},{25,17},{2,10},{10... | collective-permute-start | bytes 2359304 | tf_op jit(solution)/shard_map/ppermute | solution.py:25
  119.1 12.2 %collective-permute-start.19 = (bf16[96,4096]{1,0:T(8,128)(2,1)S(1)}, bf16[96,4096]{1,0:T(8,128)(2,1)S(1)}, u32[]{:S(2)}, u32[]{:S(2)}) collective-permute-start(bf16[96,4096]{1,0:T(8,128)(2,1)S(1)} %collective-permute-done.17.refs_1_), channel_id=1, source_target_pairs={{0,8},{8,0},{16,24},{24,16},{1,9},{9,1},{17,25},{25,17},{2,10},{10... | collective-permute-start | bytes 2359304 | tf_op jit(solution)/shard_map/ppermute | solution.py:25
  119.2 21.3 %collective-permute-start.16 = (bf16[96,4096]{1,0:T(8,128)(2,1)S(1)}, bf16[96,4096]{1,0:T(8,128)(2,1)S(1)}, u32[]{:S(2)}, u32[]{:S(2)}) collective-permute-start(bf16[96,4096]{1,0:T(8,128)(2,1)S(1)} %collective-permute-done.14.refs_5_), channel_id=1, source_target_pairs={{0,8},{8,0},{16,24},{24,16},{1,9},{9,1},{17,25},{25,17},{2,10},{10... | collective-permute-start | bytes 2359304 | tf_op jit(solution)/shard_map/ppermute | solution.py:25
  122.3 6.9 %collective-permute-start.10 = (bf16[96,1024]{1,0:T(8,128)(2,1)S(1)}, bf16[96,1024]{1,0:T(8,128)(2,1)S(1)}, u32[]{:S(2)}, u32[]{:S(2)}) collective-permute-start(bf16[96,1024]{1,0:T(8,128)(2,1)S(1)} %convolution_convert_fusion.2), channel_id=1, source_target_pairs={{0,1},{1,0},{2,3},{3,2},{4,5},{5,4},{6,7},{7,6},{8,9},{9,8},{10,11... | collective-permute-start | bytes 589832 | tf_op jit(solution)/shard_map/ppermute | solution.py:34
  129.3 1.4 collective-permute-start.22
  130.7 9.7 %collective-permute-start.12 = (bf16[96,1024]{1,0:T(8,128)(2,1)S(1)}, bf16[96,1024]{1,0:T(8,128)(2,1)S(1)}, u32[]{:S(2)}, u32[]{:S(2)}) collective-permute-start(bf16[96,1024]{1,0:T(8,128)(2,1)S(1)} %copy-done), channel_id=1, source_target_pairs={{0,8},{8,0},{16,24},{24,16},{1,9},{9,1},{17,25},{25,17},{2,10},{10... | collective-permute-start | bytes 589832 | tf_op jit(solution)/shard_map/ppermute | solution.py:25
  130.9 9.5 %collective-permute-start.13 = (bf16[96,1024]{1,0:T(8,128)(2,1)S(1)}, bf16[96,1024]{1,0:T(8,128)(2,1)S(1)}, u32[]{:S(2)}, u32[]{:S(2)}) collective-permute-start(bf16[96,1024]{1,0:T(8,128)(2,1)S(1)} %collective-permute-done.11.refs_1_), channel_id=1, source_target_pairs={{0,8},{8,0},{16,24},{24,16},{1,9},{9,1},{17,25},{25,17},{2,10},{10... | collective-permute-start | bytes 589832 | tf_op jit(solution)/shard_map/ppermute | solution.py:25

commit v3 on v2

--- a/solution.py
+++ b/solution.py
@@ -18,8 +18,16 @@
 
 
 def every_patch(group_rows, ways):
-    blocks = [group_rows]
-    bit = ways // 2
+    return finish_patches(first_patch(group_rows, ways), ways)
+
+
+def first_patch(group_rows, ways):
+    far = ways // 2
+    return [group_rows, lax.ppermute(group_rows, "ctx", [(i, i ^ far) for i in range(ways)])]
+
+
+def finish_patches(blocks, ways):
+    bit = ways // 4
     while bit:
         pairs = [(i, i ^ bit) for i in range(ways)]
         blocks = blocks + [lax.ppermute(block, "ctx", pairs) for block in blocks]
@@ -100,9 +108,9 @@
 
 def shards(n_ctx, n_row, n_col, states, context, up_weight, down_weight, cotangent):
     hidden = row_scatter(jnp.dot(context, up_weight, preferred_element_type=jnp.float32), n_row)
-    context_blocks = every_patch(context, n_ctx)
+    context_far = first_patch(context, n_ctx)
     activations = collect(jax.nn.silu(hidden).astype(jnp.bfloat16))
-    acts_blocks = every_patch(activations, n_ctx)
+    acts_far = first_patch(activations, n_ctx)
     output_terms = jnp.dot(activations, down_weight, preferred_element_type=jnp.float32)
     log_scale = jnp.tanh(feature_total(output_terms, n_col))
     shrink = jnp.exp(-log_scale)
@@ -112,19 +120,33 @@
     scale_rows = ((1.0 - cotangent_wide * flowed) * (1.0 - log_scale * log_scale)).astype(
         jnp.bfloat16
     )
+    scale_rows, acts_far, context_far = lax.optimization_barrier((scale_rows, acts_far, context_far))
     back_terms = contract(scale_rows, down_weight, 1, 1)
     back_rows = row_scatter(back_terms, n_row)
-    scale_blocks = every_patch(scale_rows, n_ctx)
-    grad_down = outer_total(acts_blocks, scale_blocks)
+    scale_far = first_patch(scale_rows, n_ctx)
+    slope_rows = (back_rows * silu_slope(hidden)).astype(jnp.bfloat16)
+    slope_rows, acts_far, scale_far, context_far = lax.optimization_barrier(
+        (slope_rows, acts_far, scale_far, context_far)
+    )
+    slope_all = collect(slope_rows)
+    slope_all, acts_far, scale_far, context_far, det_terms = lax.optimization_barrier(
+        (slope_all, acts_far, scale_far, context_far, det_terms)
+    )
+    slope_far = first_patch(slope_all, n_ctx)
+    input_terms = contract(slope_all, up_weight, 1, 1).astype(jnp.bfloat16)
+    acts_blocks = finish_patches(acts_far, n_ctx)
+    scale_blocks = finish_patches(scale_far, n_ctx)
+    context_blocks = finish_patches(context_far, n_ctx)
     if n_row == 4:
         logdet = row_pieces(det_terms, n_row)
     else:
         logdet = lax.psum_scatter(det_terms, "row", scatter_dimension=0, tiled=True)
-    slope_rows = (back_rows * silu_slope(hidden)).astype(jnp.bfloat16)
-    slope_all = collect(slope_rows)
-    slope_blocks = every_patch(slope_all, n_ctx)
-    input_terms = contract(slope_all, up_weight, 1, 1)
     grad_states = (cotangent_wide * shrink).astype(jnp.bfloat16)
+    grad_down = outer_total(acts_blocks, scale_blocks)
+    slope_far, grad_down, context_blocks, input_terms = lax.optimization_barrier(
+        (slope_far, grad_down, context_blocks, input_terms)
+    )
+    slope_blocks = finish_patches(slope_far, n_ctx)
     grad_context = feature_total(input_terms, n_col).astype(jnp.bfloat16)
     grad_up = outer_total(context_blocks, slope_blocks)
     return (flowed.astype(jnp.bfloat16), logdet, grad_states, grad_context, grad_up, grad_down)

time: 150 us -> 149 us (level)
  waiting for transfers between devices: 47.3 us -> 52.2 us
  blocking collectives: 40 us -> 35.3 us
  starting transfers between devices: 24.8 us -> 22.8 us
    ppermute x9, waiting for transfers between devices: 21.1 us -> 32.1 us  [row_pieces(): lax.ppermute(piece, 'row', [(i, (i + shift) % ways) for i in range(ways)])]
    all_gather x2, blocking collectives: 40 us -> 35.3 us  [collect(): return lax.all_gather(row_block, 'row', axis=0, tiled=True)]
    ppermute x12, waiting for transfers between devices: 17.2 us -> 13.8 us  [the longest x4 13.8 us: first_patch(): lax.ppermute(group_rows, 'ctx', [(i, i ^ far) for i in range(ways)])]
    ppermute x2, waiting for transfers between devices: 8.93 us -> 6.33 us  [feature_total(): other = lax.ppermute(sent, 'col', [(0, 1), (1, 0)])]
    ppermute x9, starting transfers between devices: 15.1 us -> 12.8 us  [row_pieces(): lax.ppermute(piece, 'row', [(i, (i + shift) % ways) for i in range(ways)])]
  transfers between devices with their start and end apart: 23 -> 23, of which waited for: 10 -> 11; matrix products, arithmetic and copies ran while one was open for 3% -> 7% of each run, Pallas kernels for 6% -> 6%
where the time goes in v3:
time: 149 us; the launch traced here: 148 us
  waiting for transfers between devices  52.2 us (35%)
  blocking collectives  35.3 us (24%)
  starting transfers between devices  22.8 us (15%)
  Pallas kernels  18.3 us (12%)
  matrix products  15.9 us (11%)
  other arithmetic  2.89 us (2%)
    all_gather x2, blocking collectives, collect(): return lax.all_gather(row_block, 'row', axis=0, tiled=True)  35.3 us
    ppermute x9, waiting for transfers between devices, row_pieces(): lax.ppermute(piece, 'row', [(i, (i + shift) % ways) for i in range(ways)])  32.1 us
    pallas_call x2, Pallas kernels, outer_total(): pl.pallas_call(functools.partial(outer_kernel, count), grid=(max(height,...  18.3 us
    ppermute x4, waiting for transfers between devices, first_patch(): lax.ppermute(group_rows, 'ctx', [(i, i ^ far) for i in range(ways)])  13.8 us
    ppermute x9, starting transfers between devices, row_pieces(): lax.ppermute(piece, 'row', [(i, (i + shift) % ways) for i in range(ways)])  12.8 us
    ppermute x2, waiting for transfers between devices, feature_total(): other = lax.ppermute(sent, 'col', [(0, 1), (1, 0)])  6.33 us
    dot_general x1, matrix products, shards(): jnp.dot(activations, down_weight, preferred_element_type=jnp.float32)  5.59 us
    dot_general x2, matrix products, contract(): lax.dot_general(left_side, right_side, (((left_dim,), (right_dim,)), ((),...  5.37 us
  transfers between devices with their start and end apart: 23, of which 11 were waited for; matrix products, arithmetic and copies ran while one was open for 7% of the time, Pallas kernels for 6%

profile of v3, /device:TPU:0, one launch (start us, length us, event | category | flops | bytes accessed | tf_op | source)
XLA Modules:
  0.0 148.4 jit_solution(4856899112370982302)
XLA Ops:
  0.7 5.0 %convolution_convert_fusion.1 = bf16[96,4096]{1,0:T(8,128)(2,1)S(1)} fusion(bf16[96,1024]{1,0:T(8,128)(2,1)} %refs_0_, bf16[1024,4096]{1,0:T(8,128)(2,1)} %param.7), kind=kOutput, calls=%fused_computation.1 | convolution fusion | flops 805699584 | bytes 9371648 | tf_op jit(solution)/shard_map/dot_general | solution.py:110
  5.7 3.1 %collective-permute-start = (bf16[24,4096]{1,0:T(8,128)(2,1)S(1)}, bf16[24,4096]{1,0:T(8,128)(2,1)S(1)}, u32[]{:S(2)}, u32[]{:S(2)}) collective-permute-start(bf16[24,4096]{1,0:T(8,128)(2,1)S(1)} %get-tuple-element.65), channel_id=1, source_target_pairs={{0,2},{2,4},{4,6},{6,0},{1,3},{3,5},{5,7},{7,1},{8,10},{10,12},{12... | collective-permute-start | bytes 589832 | tf_op jit(solution)/shard_map/ppermute | solution.py:52
  8.8 2.1 %collective-permute-start.2 = (bf16[24,4096]{1,0:T(8,128)(2,1)S(1)}, bf16[24,4096]{1,0:T(8,128)(2,1)S(1)}, u32[]{:S(2)}, u32[]{:S(2)}) collective-permute-start(bf16[24,4096]{1,0:T(8,128)(2,1)S(1)} %get-tuple-element.66), channel_id=1, source_target_pairs={{0,6},{2,0},{4,2},{6,4},{1,7},{3,1},{5,3},{7,5},{8,14},{10,8},{12,... | collective-permute-start | bytes 589832 | tf_op jit(solution)/shard_map/ppermute | solution.py:52
  10.9 0.9 collective-permute-start.1
  11.8 4.8 %collective-permute-done = bf16[24,4096]{1,0:T(8,128)(2,1)S(1)} collective-permute-done((bf16[24,4096]{1,0:T(8,128)(2,1)S(1)}, bf16[24,4096]{1,0:T(8,128)(2,1)S(1)}, u32[]{:S(2)}, u32[]{:S(2)}) %collective-permute-start) | collective-permute-done | bytes 196640 | tf_op jit(solution)/shard_map/ppermute | solution.py:52
  16.6 2.8 %collective-permute-done.2 = bf16[24,4096]{1,0:T(8,128)(2,1)S(1)} collective-permute-done((bf16[24,4096]{1,0:T(8,128)(2,1)S(1)}, bf16[24,4096]{1,0:T(8,128)(2,1)S(1)}, u32[]{:S(2)}, u32[]{:S(2)}) %collective-permute-start.2) | collective-permute-done | bytes 196640 | tf_op jit(solution)/shard_map/ppermute | solution.py:52
  19.3 9.0 %collective-permute-done.1 = bf16[24,4096]{1,0:T(8,128)(2,1)S(1)} collective-permute-done((bf16[24,4096]{1,0:T(8,128)(2,1)S(1)}, bf16[24,4096]{1,0:T(8,128)(2,1)S(1)}, u32[]{:S(2)}, u32[]{:S(2)}) %collective-permute-start.1) | collective-permute-done | bytes 196640 | tf_op jit(solution)/shard_map/ppermute | solution.py:52
  28.5 17.7 %all_gather.6.refs_0_ = bf16[96,4096]{1,0:T(8,128)(2,1)S(1)} all-gather(bf16[24,4096]{1,0:T(8,128)(2,1)S(1)} %multiply_convert_fusion.1), channel_id=1, replica_groups=mesh['ctx'=4,'row'=4,'col'=2] {'row'}, dimensions={0}, use_global_device_ids=true | all-gather | bytes 983040 | tf_op jit(solution)/shard_map/all_gather | solution.py:17
  46.3 1.6 %collective-permute-start.4 = (bf16[96,4096]{1,0:T(8,128)(2,1)S(1)}, bf16[96,4096]{1,0:T(8,128)(2,1)S(1)}, u32[]{:S(2)}, u32[]{:S(2)}) collective-permute-start(bf16[96,4096]{1,0:T(8,128)(2,1)S(1)} %all_gather.6.refs_0_), channel_id=1, source_target_pairs={{0,16},{8,24},{16,0},{24,8},{1,17},{9,25},{17,1},{25,9},{2,18},{10... | collective-permute-start | bytes 2359304 | tf_op jit(solution)/shard_map/ppermute | solution.py:26
  47.8 5.6 %convolution_convert_fusion.3 = bf16[96,1024]{1,0:T(8,128)(2,1)S(1)} fusion(bf16[96,4096]{1,0:T(8,128)(2,1)S(1)} %all_gather.6.refs_0_, bf16[4096,1024]{1,0:T(8,128)(2,1)} %param.8), kind=kOutput, calls=%fused_computation.3 | convolution fusion | flops 805404672 | bytes 9371648 | tf_op jit(solution)/shard_map/dot_general | solution.py:114
  53.4 1.6 %collective-permute-start.3 = (bf16[96,1024]{1,0:T(8,128)(2,1)S(1)}, bf16[96,1024]{1,0:T(8,128)(2,1)S(1)}, u32[]{:S(2)}, u32[]{:S(2)}) collective-permute-start(bf16[96,1024]{1,0:T(8,128)(2,1)S(1)} %convolution_convert_fusion.3), channel_id=1, source_target_pairs={{0,1},{1,0},{2,3},{3,2},{4,5},{5,4},{6,7},{7,6},{8,9},{9,8},{10,11... | collective-permute-start | bytes 589832 | tf_op jit(solution)/shard_map/ppermute | solution.py:42
  55.2 4.0 %collective-permute-done.3 = bf16[96,1024]{1,0:T(8,128)(2,1)S(1)} collective-permute-done((bf16[96,1024]{1,0:T(8,128)(2,1)S(1)}, bf16[96,1024]{1,0:T(8,128)(2,1)S(1)}, u32[]{:S(2)}, u32[]{:S(2)}) %collective-permute-start.3) | collective-permute-done | bytes 196640 | tf_op jit(solution)/shard_map/ppermute | solution.py:42
  59.2 1.1 fusion.3
  60.3 8.3 %collective-permute-done.5.refs_1_ = bf16[96,1024]{1,0:T(8,128)(2,1)S(1)} collective-permute-done((bf16[96,1024]{1,0:T(8,128)(2,1)S(1)}, bf16[96,1024]{1,0:T(8,128)(2,1)S(1)}, u32[]{:S(2)}, u32[]{:S(2)}) %collective-permute-start.5) | collective-permute-done | bytes 196640 | tf_op jit(solution)/shard_map/ppermute | solution.py:26
  68.6 2.7 %convolution_convert_fusion = bf16[96,4096]{1,0:T(8,128)(2,1)S(1)} fusion(bf16[96,1024]{1,0:T(8,128)(2,1)S(1)} %get-tuple-element.50.refs_4_, bf16[4096,1024]{1,0:T(8,128)(2,1)S(1)} %bitcast.9), kind=kOutput, calls=%fused_computation | convolution fusion | flops 805699584 | bytes 9371648 | tf_op jit(solution)/shard_map/dot_general | solution.py:65
  71.3 3.8 %collective-permute-start.8 = (bf16[24,4096]{1,0:T(8,128)(2,1)S(1)}, bf16[24,4096]{1,0:T(8,128)(2,1)S(1)}, u32[]{:S(2)}, u32[]{:S(2)}) collective-permute-start(bf16[24,4096]{1,0:T(8,128)(2,1)S(1)} %get-tuple-element.63), channel_id=1, source_target_pairs={{0,6},{2,0},{4,2},{6,4},{1,7},{3,1},{5,3},{7,5},{8,14},{10,8},{12,... | collective-permute-start | bytes 589832 | tf_op jit(solution)/shard_map/ppermute | solution.py:52
  75.2 1.5 %collective-permute-start.9 = (bf16[96,1024]{1,0:T(8,128)(2,1)S(1)}, bf16[96,1024]{1,0:T(8,128)(2,1)S(1)}, u32[]{:S(2)}, u32[]{:S(2)}) collective-permute-start(bf16[96,1024]{1,0:T(8,128)(2,1)S(1)} %get-tuple-element.50.refs_4_), channel_id=1, source_target_pairs={{0,16},{8,24},{16,0},{24,8},{1,17},{9,25},{17,1},{25,9},{2,18},{10... | collective-permute-start | bytes 589832 | tf_op jit(solution)/shard_map/ppermute | solution.py:26
  76.7 4.4 %collective-permute-done.6 = bf16[24,4096]{1,0:T(8,128)(2,1)S(1)} collective-permute-done((bf16[24,4096]{1,0:T(8,128)(2,1)S(1)}, bf16[24,4096]{1,0:T(8,128)(2,1)S(1)}, u32[]{:S(2)}, u32[]{:S(2)}) %collective-permute-start.6) | collective-permute-done | bytes 196640 | tf_op jit(solution)/shard_map/ppermute | solution.py:52
  81.1 8.4 %collective-permute-done.7 = bf16[24,4096]{1,0:T(8,128)(2,1)S(1)} collective-permute-done((bf16[24,4096]{1,0:T(8,128)(2,1)S(1)}, bf16[24,4096]{1,0:T(8,128)(2,1)S(1)}, u32[]{:S(2)}, u32[]{:S(2)}) %collective-permute-start.7) | collective-permute-done | bytes 196640 | tf_op jit(solution)/shard_map/ppermute | solution.py:52
  89.8 17.5 %all_gather.7.refs_4_ = bf16[96,4096]{1,0:T(8,128)(2,1)S(1)} all-gather(bf16[24,4096]{1,0:T(8,128)(2,1)S(1)} %multiply_convert_fusion), channel_id=1, replica_groups=mesh['ctx'=4,'row'=4,'col'=2] {'row'}, dimensions={0}, use_global_device_ids=true | all-gather | bytes 983040 | tf_op jit(solution)/shard_map/all_gather | solution.py:17
  108.4 1.5 %collective-permute-start.13 = (bf16[96,4096]{1,0:T(8,128)(2,1)S(1)}, bf16[96,4096]{1,0:T(8,128)(2,1)S(1)}, u32[]{:S(2)}, u32[]{:S(2)}) collective-permute-start(bf16[96,4096]{1,0:T(8,128)(2,1)S(1)} %all_gather.7.refs_4_), channel_id=1, source_target_pairs={{0,16},{8,24},{16,0},{24,8},{1,17},{9,25},{17,1},{25,9},{2,18},{10... | collective-permute-start | bytes 2359304 | tf_op jit(solution)/shard_map/ppermute | solution.py:26
  109.9 2.7 %convolution_convert_fusion.2 = bf16[96,1024]{1,0:T(8,128)(2,1)S(1)} fusion(bf16[96,4096]{1,0:T(8,128)(2,1)S(1)} %all_gather.7.refs_4_, bf16[1024,4096]{1,0:T(8,128)(2,1)S(1)} %bitcast.11), kind=kOutput, calls=%fused_computation.2 | convolution fusion | flops 805404672 | bytes 9371648 | tf_op jit(solution)/shard_map/dot_general | solution.py:65
  113.2 9.2 %shard_map.100 = f32[4096,1024]{1,0:T(8,128)} custom-call(bf16[96,4096]{1,0:T(8,128)(2,1)S(1)} %all_gather.6.refs_0_, bf16[96,4096]{1,0:T(8,128)(2,1)S(1)} %collective-permute-done.4.refs_1_, bf16[96,4096]{1,0:T(8,128)(2,1)S(1)} %collective-permute-done.14.refs_2_, bf16[96,4096]{1,0:T(8,128)(2,1)S(1)} %collective-permute-done.15.refs_3_, ...), custom_call_target="tpu_custom_call" | custom-call | flops 3221225472 | bytes 20709376 | tf_op jit(solution)/shard_map/pallas_call | solution.py:94
  122.3 5.5 %collective-permute-done.13.refs_5_ = bf16[96,4096]{1,0:T(8,128)(2,1)S(1)} collective-permute-done((bf16[96,4096]{1,0:T(8,128)(2,1)S(1)}, bf16[96,4096]{1,0:T(8,128)(2,1)S(1)}, u32[]{:S(2)}, u32[]{:S(2)}) %collective-permute-start.13) | collective-permute-done | bytes 786464 | tf_op jit(solution)/shard_map/ppermute | solution.py:26
  128.4 0.8 collective-permute-start.11
  129.2 1.0 collective-permute-start.12
  130.2 1.0 collective-permute-start.10
  131.3 1.6 %collective-permute-done.11 = f32[24]{0:T(128)S(1)} collective-permute-done((f32[24]{0:T(128)S(1)}, f32[24]{0:T(128)S(1)}, u32[]{:S(2)}, u32[]{:S(2)}) %collective-permute-start.11) | collective-permute-done | bytes 128 | tf_op jit(solution)/shard_map/ppermute | solution.py:52
  132.8 1.5 %collective-permute-start.20 = (bf16[96,1024]{1,0:T(8,128)(2,1)S(1)}, bf16[96,1024]{1,0:T(8,128)(2,1)S(1)}, u32[]{:S(2)}, u32[]{:S(2)}) collective-permute-start(bf16[96,1024]{1,0:T(8,128)(2,1)S(1)} %convolution_convert_fusion.2), channel_id=1, source_target_pairs={{0,1},{1,0},{2,3},{3,2},{4,5},{5,4},{6,7},{7,6},{8,9},{9,8},{10,11... | collective-permute-start | bytes 589832 | tf_op jit(solution)/shard_map/ppermute | solution.py:42
  134.4 1.2 collective-permute-done.10
  136.1 2.4 %collective-permute-done.20 = bf16[96,1024]{1,0:T(8,128)(2,1)S(1)} collective-permute-done((bf16[96,1024]{1,0:T(8,128)(2,1)S(1)}, bf16[96,1024]{1,0:T(8,128)(2,1)S(1)}, u32[]{:S(2)}, u32[]{:S(2)}) %collective-permute-start.20) | collective-permute-done | bytes 196640 | tf_op jit(solution)/shard_map/ppermute | solution.py:42
  139.2 9.2 %shard_map.101 = f32[1024,4096]{1,0:T(8,128)} custom-call(bf16[96,1024]{1,0:T(8,128)(2,1)S(1)} %copy-done, bf16[96,1024]{1,0:T(8,128)(2,1)S(1)} %collective-permute-done.5.refs_1_, bf16[96,1024]{1,0:T(8,128)(2,1)S(1)} %collective-permute-done.18.refs_2_, bf16[96,1024]{1,0:T(8,128)(2,1)S(1)} %collective-permute-done.19.refs_3_, ...), custom_call_target="tpu_custom_call" | custom-call | flops 3221225472 | bytes 20709376 | tf_op jit(solution)/shard_map/pallas_call | solution.py:94
  (47 shorter events, 4.4 us)
Async XLA Ops:
  5.7 10.9 %collective-permute-start = (bf16[24,4096]{1,0:T(8,128)(2,1)S(1)}, bf16[24,4096]{1,0:T(8,128)(2,1)S(1)}, u32[]{:S(2)}, u32[]{:S(2)}) collective-permute-start(bf16[24,4096]{1,0:T(8,128)(2,1)S(1)} %get-tuple-element.65), channel_id=1, source_target_pairs={{0,2},{2,4},{4,6},{6,0},{1,3},{3,5},{5,7},{7,1},{8,10},{10,12},{12... | collective-permute-start | bytes 589832 | tf_op jit(solution)/shard_map/ppermute | solution.py:52
  8.8 10.6 %collective-permute-start.2 = (bf16[24,4096]{1,0:T(8,128)(2,1)S(1)}, bf16[24,4096]{1,0:T(8,128)(2,1)S(1)}, u32[]{:S(2)}, u32[]{:S(2)}) collective-permute-start(bf16[24,4096]{1,0:T(8,128)(2,1)S(1)} %get-tuple-element.66), channel_id=1, source_target_pairs={{0,6},{2,0},{4,2},{6,4},{1,7},{3,1},{5,3},{7,5},{8,14},{10,8},{12,... | collective-permute-start | bytes 589832 | tf_op jit(solution)/shard_map/ppermute | solution.py:52
  10.9 17.5 %collective-permute-start.1 = (bf16[24,4096]{1,0:T(8,128)(2,1)S(1)}, bf16[24,4096]{1,0:T(8,128)(2,1)S(1)}, u32[]{:S(2)}, u32[]{:S(2)}) collective-permute-start(bf16[24,4096]{1,0:T(8,128)(2,1)S(1)} %get-tuple-element.67), channel_id=1, source_target_pairs={{0,4},{2,6},{4,0},{6,2},{1,5},{3,7},{5,1},{7,3},{8,12},{10,14},{12... | collective-permute-start | bytes 589832 | tf_op jit(solution)/shard_map/ppermute | solution.py:52
  28.5 40.0 %slice-start = ((s8[8388608]{0:T(1024)(128)(4,1)}), s8[4194304]{0:T(1024)(128)(4,1)S(1)}, s32[]{:S(2)}) async-start(s8[8388608]{0:T(1024)(128)(4,1)} %bitcast.8), calls=%async_computation | async-start | bytes 8388608
  28.5 81.3 %slice-start.2 = ((s8[8388608]{0:T(1024)(128)(4,1)}), s8[4194304]{0:T(1024)(128)(4,1)S(1)}, s32[]{:S(2)}) async-start(s8[8388608]{0:T(1024)(128)(4,1)} %bitcast.10), calls=%async_computation.2 | async-start | bytes 8388608
  46.2 8.8 %copy-start = (bf16[96,1024]{1,0:T(8,128)(2,1)S(1)}, bf16[96,1024]{1,0:T(8,128)(2,1)}, u32[]{:S(2)}) copy-start(bf16[96,1024]{1,0:T(8,128)(2,1)} %refs_0_) | copy-start | bytes 589828
  46.2 12.9 %copy-start.1 = (bf16[96,1024]{1,0:T(8,128)(2,1)S(1)}, bf16[96,1024]{1,0:T(8,128)(2,1)}, u32[]{:S(2)}) copy-start(bf16[96,1024]{1,0:T(8,128)(2,1)} %param.9) | copy-start | bytes 589828
  46.2 12.9 %copy-start.2 = (bf16[96,1024]{1,0:T(8,128)(2,1)S(1)}, bf16[96,1024]{1,0:T(8,128)(2,1)}, u32[]{:S(2)}) copy-start(bf16[96,1024]{1,0:T(8,128)(2,1)} %param.5) | copy-start | bytes 589828
  46.2 22.3 %slice-start.1 = ((s8[8388608]{0:T(1024)(128)(4,1)}), s8[4194304]{0:T(1024)(128)(4,1)S(1)}, s32[]{:S(2)}) async-start(s8[8388608]{0:T(1024)(128)(4,1)} %bitcast.8), calls=%async_computation.1 | async-start | bytes 8388608
  46.3 63.6 %slice-start.3 = ((s8[8388608]{0:T(1024)(128)(4,1)}), s8[4194304]{0:T(1024)(128)(4,1)S(1)}, s32[]{:S(2)}) async-start(s8[8388608]{0:T(1024)(128)(4,1)} %bitcast.10), calls=%async_computation.3 | async-start | bytes 8388608
  46.3 22.3 %collective-permute-start.4 = (bf16[96,4096]{1,0:T(8,128)(2,1)S(1)}, bf16[96,4096]{1,0:T(8,128)(2,1)S(1)}, u32[]{:S(2)}, u32[]{:S(2)}) collective-permute-start(bf16[96,4096]{1,0:T(8,128)(2,1)S(1)} %all_gather.6.refs_0_), channel_id=1, source_target_pairs={{0,16},{8,24},{16,0},{24,8},{1,17},{9,25},{17,1},{25,9},{2,18},{10... | collective-permute-start | bytes 2359304 | tf_op jit(solution)/shard_map/ppermute | solution.py:26
  53.4 5.7 %collective-permute-start.3 = (bf16[96,1024]{1,0:T(8,128)(2,1)S(1)}, bf16[96,1024]{1,0:T(8,128)(2,1)S(1)}, u32[]{:S(2)}, u32[]{:S(2)}) collective-permute-start(bf16[96,1024]{1,0:T(8,128)(2,1)S(1)} %convolution_convert_fusion.3), channel_id=1, source_target_pairs={{0,1},{1,0},{2,3},{3,2},{4,5},{5,4},{6,7},{7,6},{8,9},{9,8},{10,11... | collective-permute-start | bytes 589832 | tf_op jit(solution)/shard_map/ppermute | solution.py:42
  55.0 13.5 %collective-permute-start.5 = (bf16[96,1024]{1,0:T(8,128)(2,1)S(1)}, bf16[96,1024]{1,0:T(8,128)(2,1)S(1)}, u32[]{:S(2)}, u32[]{:S(2)}) collective-permute-start(bf16[96,1024]{1,0:T(8,128)(2,1)S(1)} %copy-done), channel_id=1, source_target_pairs={{0,16},{8,24},{16,0},{24,8},{1,17},{9,25},{17,1},{25,9},{2,18},{10... | collective-permute-start | bytes 589832 | tf_op jit(solution)/shard_map/ppermute | solution.py:26
  71.3 9.8 %collective-permute-start.6 = (bf16[24,4096]{1,0:T(8,128)(2,1)S(1)}, bf16[24,4096]{1,0:T(8,128)(2,1)S(1)}, u32[]{:S(2)}, u32[]{:S(2)}) collective-permute-start(bf16[24,4096]{1,0:T(8,128)(2,1)S(1)} %get-tuple-element.62), channel_id=1, source_target_pairs={{0,2},{2,4},{4,6},{6,0},{1,3},{3,5},{5,7},{7,1},{8,10},{10,12},{12... | collective-permute-start | bytes 589832 | tf_op jit(solution)/shard_map/ppermute | solution.py:52
  71.3 9.7 %collective-permute-start.8 = (bf16[24,4096]{1,0:T(8,128)(2,1)S(1)}, bf16[24,4096]{1,0:T(8,128)(2,1)S(1)}, u32[]{:S(2)}, u32[]{:S(2)}) collective-permute-start(bf16[24,4096]{1,0:T(8,128)(2,1)S(1)} %get-tuple-element.63), channel_id=1, source_target_pairs={{0,6},{2,0},{4,2},{6,4},{1,7},{3,1},{5,3},{7,5},{8,14},{10,8},{12,... | collective-permute-start | bytes 589832 | tf_op jit(solution)/shard_map/ppermute | solution.py:52
  75.2 14.3 %collective-permute-start.7 = (bf16[24,4096]{1,0:T(8,128)(2,1)S(1)}, bf16[24,4096]{1,0:T(8,128)(2,1)S(1)}, u32[]{:S(2)}, u32[]{:S(2)}) collective-permute-start(bf16[24,4096]{1,0:T(8,128)(2,1)S(1)} %get-tuple-element.64), channel_id=1, source_target_pairs={{0,4},{2,6},{4,0},{6,2},{1,5},{3,7},{5,1},{7,3},{8,12},{10,14},{12... | collective-permute-start | bytes 589832 | tf_op jit(solution)/shard_map/ppermute | solution.py:52
  75.2 14.6 %collective-permute-start.9 = (bf16[96,1024]{1,0:T(8,128)(2,1)S(1)}, bf16[96,1024]{1,0:T(8,128)(2,1)S(1)}, u32[]{:S(2)}, u32[]{:S(2)}) collective-permute-start(bf16[96,1024]{1,0:T(8,128)(2,1)S(1)} %get-tuple-element.50.refs_4_), channel_id=1, source_target_pairs={{0,16},{8,24},{16,0},{24,8},{1,17},{9,25},{17,1},{25,9},{2,18},{10... | collective-permute-start | bytes 589832 | tf_op jit(solution)/shard_map/ppermute | solution.py:26
  107.3 5.8 %collective-permute-start.14 = (bf16[96,4096]{1,0:T(8,128)(2,1)S(1)}, bf16[96,4096]{1,0:T(8,128)(2,1)S(1)}, u32[]{:S(2)}, u32[]{:S(2)}) collective-permute-start(bf16[96,4096]{1,0:T(8,128)(2,1)S(1)} %all_gather.6.refs_0_), channel_id=1, source_target_pairs={{0,8},{8,0},{16,24},{24,16},{1,9},{9,1},{17,25},{25,17},{2,10},{10... | collective-permute-start | bytes 2359304 | tf_op jit(solution)/shard_map/ppermute | solution.py:33
  107.3 5.8 %collective-permute-start.15 = (bf16[96,4096]{1,0:T(8,128)(2,1)S(1)}, bf16[96,4096]{1,0:T(8,128)(2,1)S(1)}, u32[]{:S(2)}, u32[]{:S(2)}) collective-permute-start(bf16[96,4096]{1,0:T(8,128)(2,1)S(1)} %collective-permute-done.4.refs_1_), channel_id=1, source_target_pairs={{0,8},{8,0},{16,24},{24,16},{1,9},{9,1},{17,25},{25,17},{2,10},{10... | collective-permute-start | bytes 2359304 | tf_op jit(solution)/shard_map/ppermute | solution.py:33
  107.8 4.7 %collective-permute-start.16 = (bf16[96,1024]{1,0:T(8,128)(2,1)S(1)}, bf16[96,1024]{1,0:T(8,128)(2,1)S(1)}, u32[]{:S(2)}, u32[]{:S(2)}) collective-permute-start(bf16[96,1024]{1,0:T(8,128)(2,1)S(1)} %get-tuple-element.50.refs_4_), channel_id=1, source_target_pairs={{0,8},{8,0},{16,24},{24,16},{1,9},{9,1},{17,25},{25,17},{2,10},{10... | collective-permute-start | bytes 589832 | tf_op jit(solution)/shard_map/ppermute | solution.py:33
  107.8 4.8 %collective-permute-start.17 = (bf16[96,1024]{1,0:T(8,128)(2,1)S(1)}, bf16[96,1024]{1,0:T(8,128)(2,1)S(1)}, u32[]{:S(2)}, u32[]{:S(2)}) collective-permute-start(bf16[96,1024]{1,0:T(8,128)(2,1)S(1)} %collective-permute-done.9.refs_5_), channel_id=1, source_target_pairs={{0,8},{8,0},{16,24},{24,16},{1,9},{9,1},{17,25},{25,17},{2,10},{10... | collective-permute-start | bytes 589832 | tf_op jit(solution)/shard_map/ppermute | solution.py:33
  108.4 19.4 %collective-permute-start.13 = (bf16[96,4096]{1,0:T(8,128)(2,1)S(1)}, bf16[96,4096]{1,0:T(8,128)(2,1)S(1)}, u32[]{:S(2)}, u32[]{:S(2)}) collective-permute-start(bf16[96,4096]{1,0:T(8,128)(2,1)S(1)} %all_gather.7.refs_4_), channel_id=1, source_target_pairs={{0,16},{8,24},{16,0},{24,8},{1,17},{9,25},{17,1},{25,9},{2,18},{10... | collective-permute-start | bytes 2359304 | tf_op jit(solution)/shard_map/ppermute | solution.py:26
  112.6 9.7 %collective-permute-start.18 = (bf16[96,1024]{1,0:T(8,128)(2,1)S(1)}, bf16[96,1024]{1,0:T(8,128)(2,1)S(1)}, u32[]{:S(2)}, u32[]{:S(2)}) collective-permute-start(bf16[96,1024]{1,0:T(8,128)(2,1)S(1)} %copy-done), channel_id=1, source_target_pairs={{0,8},{8,0},{16,24},{24,16},{1,9},{9,1},{17,25},{25,17},{2,10},{10... | collective-permute-start | bytes 589832 | tf_op jit(solution)/shard_map/ppermute | solution.py:33
  112.7 9.7 %collective-permute-start.19 = (bf16[96,1024]{1,0:T(8,128)(2,1)S(1)}, bf16[96,1024]{1,0:T(8,128)(2,1)S(1)}, u32[]{:S(2)}, u32[]{:S(2)}) collective-permute-start(bf16[96,1024]{1,0:T(8,128)(2,1)S(1)} %collective-permute-done.5.refs_1_), channel_id=1, source_target_pairs={{0,8},{8,0},{16,24},{24,16},{1,9},{9,1},{17,25},{25,17},{2,10},{10... | collective-permute-start | bytes 589832 | tf_op jit(solution)/shard_map/ppermute | solution.py:33
  127.8 11.4 %collective-permute-start.21 = (bf16[96,4096]{1,0:T(8,128)(2,1)S(1)}, bf16[96,4096]{1,0:T(8,128)(2,1)S(1)}, u32[]{:S(2)}, u32[]{:S(2)}) collective-permute-start(bf16[96,4096]{1,0:T(8,128)(2,1)S(1)} %all_gather.7.refs_4_), channel_id=1, source_target_pairs={{0,8},{8,0},{16,24},{24,16},{1,9},{9,1},{17,25},{25,17},{2,10},{10... | collective-permute-start | bytes 2359304 | tf_op jit(solution)/shard_map/ppermute | solution.py:33
  127.8 11.4 %collective-permute-start.22 = (bf16[96,4096]{1,0:T(8,128)(2,1)S(1)}, bf16[96,4096]{1,0:T(8,128)(2,1)S(1)}, u32[]{:S(2)}, u32[]{:S(2)}) collective-permute-start(bf16[96,4096]{1,0:T(8,128)(2,1)S(1)} %collective-permute-done.13.refs_5_), channel_id=1, source_target_pairs={{0,8},{8,0},{16,24},{24,16},{1,9},{9,1},{17,25},{25,17},{2,10},{10... | collective-permute-start | bytes 2359304 | tf_op jit(solution)/shard_map/ppermute | solution.py:33
  128.4 4.4 %collective-permute-start.11 = (f32[24]{0:T(128)S(1)}, f32[24]{0:T(128)S(1)}, u32[]{:S(2)}, u32[]{:S(2)}) collective-permute-start(f32[24]{0:T(128)S(1)} %get-tuple-element.72), channel_id=1, source_target_pairs={{0,4},{2,6},{4,0},{6,2},{1,5},{3,7},{5,1},{7,3},{8,12},{10,14},{12... | collective-permute-start | bytes 296 | tf_op jit(solution)/shard_map/ppermute | solution.py:52
  129.2 5.1 %collective-permute-start.12 = (f32[24]{0:T(128)S(1)}, f32[24]{0:T(128)S(1)}, u32[]{:S(2)}, u32[]{:S(2)}) collective-permute-start(f32[24]{0:T(128)S(1)} %get-tuple-element.73), channel_id=1, source_target_pairs={{0,6},{2,0},{4,2},{6,4},{1,7},{3,1},{5,3},{7,5},{8,14},{10,8},{12,... | collective-permute-start | bytes 296 | tf_op jit(solution)/shard_map/ppermute | solution.py:52
  130.2 5.3 %collective-permute-start.10 = (f32[24]{0:T(128)S(1)}, f32[24]{0:T(128)S(1)}, u32[]{:S(2)}, u32[]{:S(2)}) collective-permute-start(f32[24]{0:T(128)S(1)} %get-tuple-element.74), channel_id=1, source_target_pairs={{0,2},{2,4},{4,6},{6,0},{1,3},{3,5},{5,7},{7,1},{8,10},{10,12},{12... | collective-permute-start | bytes 296 | tf_op jit(solution)/shard_map/ppermute | solution.py:52
  132.8 5.7 %collective-permute-start.20 = (bf16[96,1024]{1,0:T(8,128)(2,1)S(1)}, bf16[96,1024]{1,0:T(8,128)(2,1)S(1)}, u32[]{:S(2)}, u32[]{:S(2)}) collective-permute-start(bf16[96,1024]{1,0:T(8,128)(2,1)S(1)} %convolution_convert_fusion.2), channel_id=1, source_target_pairs={{0,1},{1,0},{2,3},{3,2},{4,5},{5,4},{6,7},{7,6},{8,9},{9,8},{10,11... | collective-permute-start | bytes 589832 | tf_op jit(solution)/shard_map/ppermute | solution.py:42

commit v4 on v3

--- a/solution.py
+++ b/solution.py
@@ -143,11 +143,11 @@
         logdet = lax.psum_scatter(det_terms, "row", scatter_dimension=0, tiled=True)
     grad_states = (cotangent_wide * shrink).astype(jnp.bfloat16)
     grad_down = outer_total(acts_blocks, scale_blocks)
-    slope_far, grad_down, context_blocks, input_terms = lax.optimization_barrier(
-        (slope_far, grad_down, context_blocks, input_terms)
+    grad_context = feature_total(input_terms, n_col).astype(jnp.bfloat16)
+    slope_far, grad_down, context_blocks, grad_context, logdet = lax.optimization_barrier(
+        (slope_far, grad_down, context_blocks, grad_context, logdet)
     )
     slope_blocks = finish_patches(slope_far, n_ctx)
-    grad_context = feature_total(input_terms, n_col).astype(jnp.bfloat16)
     grad_up = outer_total(context_blocks, slope_blocks)
     return (flowed.astype(jnp.bfloat16), logdet, grad_states, grad_context, grad_up, grad_down)
 

time: 149 us -> 147 us (0.987)
    ppermute x4, waiting for transfers between devices: 13.8 us -> 8.29 us  [first_patch(): lax.ppermute(group_rows, 'ctx', [(i, i ^ far) for i in range(ways)])]
    ppermute x9, waiting for transfers between devices: 32.1 us -> 35.8 us  [row_pieces(): lax.ppermute(piece, 'row', [(i, (i + shift) % ways) for i in range(ways)])]
    ppermute x8, waiting for transfers between devices: 0.02 us -> 3.25 us  [finish_patches(): blocks = blocks + [lax.ppermute(block, 'ctx', pairs) for block in blocks]]
    ppermute x2, waiting for transfers between devices: 6.33 us -> 3.96 us  [feature_total(): other = lax.ppermute(sent, 'col', [(0, 1), (1, 0)])]
  transfers between devices with their start and end apart: 23 -> 23, of which waited for: 11 -> 12; matrix products, arithmetic and copies ran while one was open for 7% -> 8% of each run, Pallas kernels for 6% -> 6%
where the time goes in v4:
time: 147 us; the launch traced here: 146 us
  waiting for transfers between devices  51.3 us (35%)
  blocking collectives  35.3 us (24%)
  starting transfers between devices  21.7 us (15%)
  Pallas kernels  18.3 us (12%)
  matrix products  15.9 us (11%)
  other arithmetic  2.89 us (2%)
    ppermute x9, waiting for transfers between devices, row_pieces(): lax.ppermute(piece, 'row', [(i, (i + shift) % ways) for i in range(ways)])  35.8 us
    all_gather x2, blocking collectives, collect(): return lax.all_gather(row_block, 'row', axis=0, tiled=True)  35.3 us
    pallas_call x2, Pallas kernels, outer_total(): pl.pallas_call(functools.partial(outer_kernel, count), grid=(max(height,...  18.3 us
    ppermute x9, starting transfers between devices, row_pieces(): lax.ppermute(piece, 'row', [(i, (i + shift) % ways) for i in range(ways)])  11.8 us
    ppermute x4, waiting for transfers between devices, first_patch(): lax.ppermute(group_rows, 'ctx', [(i, i ^ far) for i in range(ways)])  8.29 us
    dot_general x1, matrix products, shards(): jnp.dot(activations, down_weight, preferred_element_type=jnp.float32)  5.59 us
    dot_general x2, matrix products, contract(): lax.dot_general(left_side, right_side, (((left_dim,), (right_dim,)), ((),...  5.37 us
    dot_general x1, matrix products, shards(): jnp.dot(context, up_weight, preferred_element_type=jnp.float32)  4.95 us
  transfers between devices with their start and end apart: 23, of which 12 were waited for; matrix products, arithmetic and copies ran while one was open for 8% of the time, Pallas kernels for 6%

profile of v4, /device:TPU:0, one launch (start us, length us, event | category | flops | bytes accessed | tf_op | source)
XLA Modules:
  0.0 146.4 jit_solution(17225810079723070336)
XLA Ops:
  0.7 5.0 %convolution_convert_fusion.1 = bf16[96,4096]{1,0:T(8,128)(2,1)S(1)} fusion(bf16[96,1024]{1,0:T(8,128)(2,1)} %refs_0_, bf16[1024,4096]{1,0:T(8,128)(2,1)} %param.7), kind=kOutput, calls=%fused_computation.1 | convolution fusion | flops 805699584 | bytes 9371648 | tf_op jit(solution)/shard_map/dot_general | solution.py:110
  5.7 3.1 %collective-permute-start = (bf16[24,4096]{1,0:T(8,128)(2,1)S(1)}, bf16[24,4096]{1,0:T(8,128)(2,1)S(1)}, u32[]{:S(2)}, u32[]{:S(2)}) collective-permute-start(bf16[24,4096]{1,0:T(8,128)(2,1)S(1)} %get-tuple-element.67), channel_id=1, source_target_pairs={{0,2},{2,4},{4,6},{6,0},{1,3},{3,5},{5,7},{7,1},{8,10},{10,12},{12... | collective-permute-start | bytes 589832 | tf_op jit(solution)/shard_map/ppermute | solution.py:52
  8.8 2.1 %collective-permute-start.2 = (bf16[24,4096]{1,0:T(8,128)(2,1)S(1)}, bf16[24,4096]{1,0:T(8,128)(2,1)S(1)}, u32[]{:S(2)}, u32[]{:S(2)}) collective-permute-start(bf16[24,4096]{1,0:T(8,128)(2,1)S(1)} %get-tuple-element.68), channel_id=1, source_target_pairs={{0,6},{2,0},{4,2},{6,4},{1,7},{3,1},{5,3},{7,5},{8,14},{10,8},{12,... | collective-permute-start | bytes 589832 | tf_op jit(solution)/shard_map/ppermute | solution.py:52
  10.9 0.9 collective-permute-start.1
  11.8 4.8 %collective-permute-done = bf16[24,4096]{1,0:T(8,128)(2,1)S(1)} collective-permute-done((bf16[24,4096]{1,0:T(8,128)(2,1)S(1)}, bf16[24,4096]{1,0:T(8,128)(2,1)S(1)}, u32[]{:S(2)}, u32[]{:S(2)}) %collective-permute-start) | collective-permute-done | bytes 196640 | tf_op jit(solution)/shard_map/ppermute | solution.py:52
  16.6 2.8 %collective-permute-done.2 = bf16[24,4096]{1,0:T(8,128)(2,1)S(1)} collective-permute-done((bf16[24,4096]{1,0:T(8,128)(2,1)S(1)}, bf16[24,4096]{1,0:T(8,128)(2,1)S(1)}, u32[]{:S(2)}, u32[]{:S(2)}) %collective-permute-start.2) | collective-permute-done | bytes 196640 | tf_op jit(solution)/shard_map/ppermute | solution.py:52
  19.3 9.0 %collective-permute-done.1 = bf16[24,4096]{1,0:T(8,128)(2,1)S(1)} collective-permute-done((bf16[24,4096]{1,0:T(8,128)(2,1)S(1)}, bf16[24,4096]{1,0:T(8,128)(2,1)S(1)}, u32[]{:S(2)}, u32[]{:S(2)}) %collective-permute-start.1) | collective-permute-done | bytes 196640 | tf_op jit(solution)/shard_map/ppermute | solution.py:52
  28.5 17.7 %all_gather.6.refs_0_ = bf16[96,4096]{1,0:T(8,128)(2,1)S(1)} all-gather(bf16[24,4096]{1,0:T(8,128)(2,1)S(1)} %multiply_convert_fusion.1), channel_id=1, replica_groups=mesh['ctx'=4,'row'=4,'col'=2] {'row'}, dimensions={0}, use_global_device_ids=true | all-gather | bytes 983040 | tf_op jit(solution)/shard_map/all_gather | solution.py:17
  46.3 1.6 %collective-permute-start.4 = (bf16[96,4096]{1,0:T(8,128)(2,1)S(1)}, bf16[96,4096]{1,0:T(8,128)(2,1)S(1)}, u32[]{:S(2)}, u32[]{:S(2)}) collective-permute-start(bf16[96,4096]{1,0:T(8,128)(2,1)S(1)} %all_gather.6.refs_0_), channel_id=1, source_target_pairs={{0,16},{8,24},{16,0},{24,8},{1,17},{9,25},{17,1},{25,9},{2,18},{10... | collective-permute-start | bytes 2359304 | tf_op jit(solution)/shard_map/ppermute | solution.py:26
  47.8 5.6 %convolution_convert_fusion.3 = bf16[96,1024]{1,0:T(8,128)(2,1)S(1)} fusion(bf16[96,4096]{1,0:T(8,128)(2,1)S(1)} %all_gather.6.refs_0_, bf16[4096,1024]{1,0:T(8,128)(2,1)} %param.8), kind=kOutput, calls=%fused_computation.3 | convolution fusion | flops 805404672 | bytes 9371648 | tf_op jit(solution)/shard_map/dot_general | solution.py:114
  53.4 1.6 %collective-permute-start.3 = (bf16[96,1024]{1,0:T(8,128)(2,1)S(1)}, bf16[96,1024]{1,0:T(8,128)(2,1)S(1)}, u32[]{:S(2)}, u32[]{:S(2)}) collective-permute-start(bf16[96,1024]{1,0:T(8,128)(2,1)S(1)} %convolution_convert_fusion.3), channel_id=1, source_target_pairs={{0,1},{1,0},{2,3},{3,2},{4,5},{5,4},{6,7},{7,6},{8,9},{9,8},{10,11... | collective-permute-start | bytes 589832 | tf_op jit(solution)/shard_map/ppermute | solution.py:42
  55.2 4.0 %collective-permute-done.3 = bf16[96,1024]{1,0:T(8,128)(2,1)S(1)} collective-permute-done((bf16[96,1024]{1,0:T(8,128)(2,1)S(1)}, bf16[96,1024]{1,0:T(8,128)(2,1)S(1)}, u32[]{:S(2)}, u32[]{:S(2)}) %collective-permute-start.3) | collective-permute-done | bytes 196640 | tf_op jit(solution)/shard_map/ppermute | solution.py:42
  59.2 1.1 fusion.3
  60.3 8.3 %collective-permute-done.5.refs_1_ = bf16[96,1024]{1,0:T(8,128)(2,1)S(1)} collective-permute-done((bf16[96,1024]{1,0:T(8,128)(2,1)S(1)}, bf16[96,1024]{1,0:T(8,128)(2,1)S(1)}, u32[]{:S(2)}, u32[]{:S(2)}) %collective-permute-start.5) | collective-permute-done | bytes 196640 | tf_op jit(solution)/shard_map/ppermute | solution.py:26
  68.6 2.7 %convolution_convert_fusion = bf16[96,4096]{1,0:T(8,128)(2,1)S(1)} fusion(bf16[96,1024]{1,0:T(8,128)(2,1)S(1)} %get-tuple-element.50.refs_4_, bf16[4096,1024]{1,0:T(8,128)(2,1)S(1)} %bitcast.9), kind=kOutput, calls=%fused_computation | convolution fusion | flops 805699584 | bytes 9371648 | tf_op jit(solution)/shard_map/dot_general | solution.py:65
  71.3 3.8 %collective-permute-start.8 = (bf16[24,4096]{1,0:T(8,128)(2,1)S(1)}, bf16[24,4096]{1,0:T(8,128)(2,1)S(1)}, u32[]{:S(2)}, u32[]{:S(2)}) collective-permute-start(bf16[24,4096]{1,0:T(8,128)(2,1)S(1)} %get-tuple-element.65), channel_id=1, source_target_pairs={{0,6},{2,0},{4,2},{6,4},{1,7},{3,1},{5,3},{7,5},{8,14},{10,8},{12,... | collective-permute-start | bytes 589832 | tf_op jit(solution)/shard_map/ppermute | solution.py:52
  75.2 1.5 %collective-permute-start.9 = (bf16[96,1024]{1,0:T(8,128)(2,1)S(1)}, bf16[96,1024]{1,0:T(8,128)(2,1)S(1)}, u32[]{:S(2)}, u32[]{:S(2)}) collective-permute-start(bf16[96,1024]{1,0:T(8,128)(2,1)S(1)} %get-tuple-element.50.refs_4_), channel_id=1, source_target_pairs={{0,16},{8,24},{16,0},{24,8},{1,17},{9,25},{17,1},{25,9},{2,18},{10... | collective-permute-start | bytes 589832 | tf_op jit(solution)/shard_map/ppermute | solution.py:26
  76.7 4.4 %collective-permute-done.6 = bf16[24,4096]{1,0:T(8,128)(2,1)S(1)} collective-permute-done((bf16[24,4096]{1,0:T(8,128)(2,1)S(1)}, bf16[24,4096]{1,0:T(8,128)(2,1)S(1)}, u32[]{:S(2)}, u32[]{:S(2)}) %collective-permute-start.6) | collective-permute-done | bytes 196640 | tf_op jit(solution)/shard_map/ppermute | solution.py:52
  81.1 8.4 %collective-permute-done.7 = bf16[24,4096]{1,0:T(8,128)(2,1)S(1)} collective-permute-done((bf16[24,4096]{1,0:T(8,128)(2,1)S(1)}, bf16[24,4096]{1,0:T(8,128)(2,1)S(1)}, u32[]{:S(2)}, u32[]{:S(2)}) %collective-permute-start.7) | collective-permute-done | bytes 196640 | tf_op jit(solution)/shard_map/ppermute | solution.py:52
  89.8 17.5 %all_gather.7.refs_4_ = bf16[96,4096]{1,0:T(8,128)(2,1)S(1)} all-gather(bf16[24,4096]{1,0:T(8,128)(2,1)S(1)} %multiply_convert_fusion), channel_id=1, replica_groups=mesh['ctx'=4,'row'=4,'col'=2] {'row'}, dimensions={0}, use_global_device_ids=true | all-gather | bytes 983040 | tf_op jit(solution)/shard_map/all_gather | solution.py:17
  107.9 2.7 %convolution_convert_fusion.2 = bf16[96,1024]{1,0:T(8,128)(2,1)S(1)} fusion(bf16[96,4096]{1,0:T(8,128)(2,1)S(1)} %all_gather.7.refs_4_, bf16[1024,4096]{1,0:T(8,128)(2,1)S(1)} %bitcast.11), kind=kOutput, calls=%fused_computation.2 | convolution fusion | flops 805404672 | bytes 9371648 | tf_op jit(solution)/shard_map/dot_general | solution.py:65
  110.6 1.6 %collective-permute-start.10 = (bf16[96,4096]{1,0:T(8,128)(2,1)S(1)}, bf16[96,4096]{1,0:T(8,128)(2,1)S(1)}, u32[]{:S(2)}, u32[]{:S(2)}) collective-permute-start(bf16[96,4096]{1,0:T(8,128)(2,1)S(1)} %all_gather.7.refs_4_), channel_id=1, source_target_pairs={{0,16},{8,24},{16,0},{24,8},{1,17},{9,25},{17,1},{25,9},{2,18},{10... | collective-permute-start | bytes 2359304 | tf_op jit(solution)/shard_map/ppermute | solution.py:26
  112.2 0.8 collective-permute-start.19
  113.0 1.0 collective-permute-start.20
  114.0 2.6 %collective-permute-done.19 = f32[24]{0:T(128)S(1)} collective-permute-done((f32[24]{0:T(128)S(1)}, f32[24]{0:T(128)S(1)}, u32[]{:S(2)}, u32[]{:S(2)}) %collective-permute-start.19) | collective-permute-done | bytes 128 | tf_op jit(solution)/shard_map/ppermute | solution.py:52
  116.7 1.5 %collective-permute-start.17 = (bf16[96,1024]{1,0:T(8,128)(2,1)S(1)}, bf16[96,1024]{1,0:T(8,128)(2,1)S(1)}, u32[]{:S(2)}, u32[]{:S(2)}) collective-permute-start(bf16[96,1024]{1,0:T(8,128)(2,1)S(1)} %convolution_convert_fusion.2), channel_id=1, source_target_pairs={{0,1},{1,0},{2,3},{3,2},{4,5},{5,4},{6,7},{7,6},{8,9},{9,8},{10,11... | collective-permute-start | bytes 589832 | tf_op jit(solution)/shard_map/ppermute | solution.py:42
  118.2 3.8 %collective-permute-done.18 = f32[24]{0:T(128)S(1)} collective-permute-done((f32[24]{0:T(128)S(1)}, f32[24]{0:T(128)S(1)}, u32[]{:S(2)}, u32[]{:S(2)}) %collective-permute-start.18) | collective-permute-done | bytes 128 | tf_op jit(solution)/shard_map/ppermute | solution.py:52
  123.1 0.7 add_convert_fusion
  124.5 9.2 %shard_map.100 = f32[4096,1024]{1,0:T(8,128)} custom-call(bf16[96,4096]{1,0:T(8,128)(2,1)S(1)} %all_gather.6.refs_0_, bf16[96,4096]{1,0:T(8,128)(2,1)S(1)} %collective-permute-done.4.refs_1_, bf16[96,4096]{1,0:T(8,128)(2,1)S(1)} %collective-permute-done.11.refs_2_, bf16[96,4096]{1,0:T(8,128)(2,1)S(1)} %collective-permute-done.12.refs_3_, ...), custom_call_target="tpu_custom_call" | custom-call | flops 3221225472 | bytes 20709376 | tf_op jit(solution)/shard_map/pallas_call | solution.py:94
  134.3 1.8 %collective-permute-done.21.refs_6_ = bf16[96,4096]{1,0:T(8,128)(2,1)S(1)} collective-permute-done((bf16[96,4096]{1,0:T(8,128)(2,1)S(1)}, bf16[96,4096]{1,0:T(8,128)(2,1)S(1)}, u32[]{:S(2)}, u32[]{:S(2)}) %collective-permute-start.21) | collective-permute-done | bytes 786464 | tf_op jit(solution)/shard_map/ppermute | solution.py:33
  136.1 1.1 collective-permute-done.22.refs_7_
  137.2 9.2 %shard_map.101 = f32[1024,4096]{1,0:T(8,128)} custom-call(bf16[96,1024]{1,0:T(8,128)(2,1)S(1)} %copy-done, bf16[96,1024]{1,0:T(8,128)(2,1)S(1)} %collective-permute-done.5.refs_1_, bf16[96,1024]{1,0:T(8,128)(2,1)S(1)} %collective-permute-done.15.refs_2_, bf16[96,1024]{1,0:T(8,128)(2,1)S(1)} %collective-permute-done.16.refs_3_, ...), custom_call_target="tpu_custom_call" | custom-call | flops 3221225472 | bytes 20709376 | tf_op jit(solution)/shard_map/pallas_call | solution.py:94
  (47 shorter events, 3.9 us)
Async XLA Ops:
  5.7 10.9 %collective-permute-start = (bf16[24,4096]{1,0:T(8,128)(2,1)S(1)}, bf16[24,4096]{1,0:T(8,128)(2,1)S(1)}, u32[]{:S(2)}, u32[]{:S(2)}) collective-permute-start(bf16[24,4096]{1,0:T(8,128)(2,1)S(1)} %get-tuple-element.67), channel_id=1, source_target_pairs={{0,2},{2,4},{4,6},{6,0},{1,3},{3,5},{5,7},{7,1},{8,10},{10,12},{12... | collective-permute-start | bytes 589832 | tf_op jit(solution)/shard_map/ppermute | solution.py:52
  8.8 10.6 %collective-permute-start.2 = (bf16[24,4096]{1,0:T(8,128)(2,1)S(1)}, bf16[24,4096]{1,0:T(8,128)(2,1)S(1)}, u32[]{:S(2)}, u32[]{:S(2)}) collective-permute-start(bf16[24,4096]{1,0:T(8,128)(2,1)S(1)} %get-tuple-element.68), channel_id=1, source_target_pairs={{0,6},{2,0},{4,2},{6,4},{1,7},{3,1},{5,3},{7,5},{8,14},{10,8},{12,... | collective-permute-start | bytes 589832 | tf_op jit(solution)/shard_map/ppermute | solution.py:52
  10.9 17.5 %collective-permute-start.1 = (bf16[24,4096]{1,0:T(8,128)(2,1)S(1)}, bf16[24,4096]{1,0:T(8,128)(2,1)S(1)}, u32[]{:S(2)}, u32[]{:S(2)}) collective-permute-start(bf16[24,4096]{1,0:T(8,128)(2,1)S(1)} %get-tuple-element.69), channel_id=1, source_target_pairs={{0,4},{2,6},{4,0},{6,2},{1,5},{3,7},{5,1},{7,3},{8,12},{10,14},{12... | collective-permute-start | bytes 589832 | tf_op jit(solution)/shard_map/ppermute | solution.py:52
  28.5 40.0 %slice-start = ((s8[8388608]{0:T(1024)(128)(4,1)}), s8[4194304]{0:T(1024)(128)(4,1)S(1)}, s32[]{:S(2)}) async-start(s8[8388608]{0:T(1024)(128)(4,1)} %bitcast.8), calls=%async_computation | async-start | bytes 8388608
  28.5 79.3 %slice-start.2 = ((s8[8388608]{0:T(1024)(128)(4,1)}), s8[4194304]{0:T(1024)(128)(4,1)S(1)}, s32[]{:S(2)}) async-start(s8[8388608]{0:T(1024)(128)(4,1)} %bitcast.10), calls=%async_computation.2 | async-start | bytes 8388608
  46.2 8.8 %copy-start = (bf16[96,1024]{1,0:T(8,128)(2,1)S(1)}, bf16[96,1024]{1,0:T(8,128)(2,1)}, u32[]{:S(2)}) copy-start(bf16[96,1024]{1,0:T(8,128)(2,1)} %refs_0_) | copy-start | bytes 589828
  46.2 12.9 %copy-start.1 = (bf16[96,1024]{1,0:T(8,128)(2,1)S(1)}, bf16[96,1024]{1,0:T(8,128)(2,1)}, u32[]{:S(2)}) copy-start(bf16[96,1024]{1,0:T(8,128)(2,1)} %param.9) | copy-start | bytes 589828
  46.2 12.9 %copy-start.2 = (bf16[96,1024]{1,0:T(8,128)(2,1)S(1)}, bf16[96,1024]{1,0:T(8,128)(2,1)}, u32[]{:S(2)}) copy-start(bf16[96,1024]{1,0:T(8,128)(2,1)} %param.5) | copy-start | bytes 589828
  46.2 22.3 %slice-start.1 = ((s8[8388608]{0:T(1024)(128)(4,1)}), s8[4194304]{0:T(1024)(128)(4,1)S(1)}, s32[]{:S(2)}) async-start(s8[8388608]{0:T(1024)(128)(4,1)} %bitcast.8), calls=%async_computation.1 | async-start | bytes 8388608
  46.3 61.6 %slice-start.3 = ((s8[8388608]{0:T(1024)(128)(4,1)}), s8[4194304]{0:T(1024)(128)(4,1)S(1)}, s32[]{:S(2)}) async-start(s8[8388608]{0:T(1024)(128)(4,1)} %bitcast.10), calls=%async_computation.3 | async-start | bytes 8388608
  46.3 22.3 %collective-permute-start.4 = (bf16[96,4096]{1,0:T(8,128)(2,1)S(1)}, bf16[96,4096]{1,0:T(8,128)(2,1)S(1)}, u32[]{:S(2)}, u32[]{:S(2)}) collective-permute-start(bf16[96,4096]{1,0:T(8,128)(2,1)S(1)} %all_gather.6.refs_0_), channel_id=1, source_target_pairs={{0,16},{8,24},{16,0},{24,8},{1,17},{9,25},{17,1},{25,9},{2,18},{10... | collective-permute-start | bytes 2359304 | tf_op jit(solution)/shard_map/ppermute | solution.py:26
  53.4 5.7 %collective-permute-start.3 = (bf16[96,1024]{1,0:T(8,128)(2,1)S(1)}, bf16[96,1024]{1,0:T(8,128)(2,1)S(1)}, u32[]{:S(2)}, u32[]{:S(2)}) collective-permute-start(bf16[96,1024]{1,0:T(8,128)(2,1)S(1)} %convolution_convert_fusion.3), channel_id=1, source_target_pairs={{0,1},{1,0},{2,3},{3,2},{4,5},{5,4},{6,7},{7,6},{8,9},{9,8},{10,11... | collective-permute-start | bytes 589832 | tf_op jit(solution)/shard_map/ppermute | solution.py:42
  55.0 13.5 %collective-permute-start.5 = (bf16[96,1024]{1,0:T(8,128)(2,1)S(1)}, bf16[96,1024]{1,0:T(8,128)(2,1)S(1)}, u32[]{:S(2)}, u32[]{:S(2)}) collective-permute-start(bf16[96,1024]{1,0:T(8,128)(2,1)S(1)} %copy-done), channel_id=1, source_target_pairs={{0,16},{8,24},{16,0},{24,8},{1,17},{9,25},{17,1},{25,9},{2,18},{10... | collective-permute-start | bytes 589832 | tf_op jit(solution)/shard_map/ppermute | solution.py:26
  71.3 9.8 %collective-permute-start.6 = (bf16[24,4096]{1,0:T(8,128)(2,1)S(1)}, bf16[24,4096]{1,0:T(8,128)(2,1)S(1)}, u32[]{:S(2)}, u32[]{:S(2)}) collective-permute-start(bf16[24,4096]{1,0:T(8,128)(2,1)S(1)} %get-tuple-element.64), channel_id=1, source_target_pairs={{0,2},{2,4},{4,6},{6,0},{1,3},{3,5},{5,7},{7,1},{8,10},{10,12},{12... | collective-permute-start | bytes 589832 | tf_op jit(solution)/shard_map/ppermute | solution.py:52
  71.3 9.7 %collective-permute-start.8 = (bf16[24,4096]{1,0:T(8,128)(2,1)S(1)}, bf16[24,4096]{1,0:T(8,128)(2,1)S(1)}, u32[]{:S(2)}, u32[]{:S(2)}) collective-permute-start(bf16[24,4096]{1,0:T(8,128)(2,1)S(1)} %get-tuple-element.65), channel_id=1, source_target_pairs={{0,6},{2,0},{4,2},{6,4},{1,7},{3,1},{5,3},{7,5},{8,14},{10,8},{12,... | collective-permute-start | bytes 589832 | tf_op jit(solution)/shard_map/ppermute | solution.py:52
  75.2 14.3 %collective-permute-start.7 = (bf16[24,4096]{1,0:T(8,128)(2,1)S(1)}, bf16[24,4096]{1,0:T(8,128)(2,1)S(1)}, u32[]{:S(2)}, u32[]{:S(2)}) collective-permute-start(bf16[24,4096]{1,0:T(8,128)(2,1)S(1)} %get-tuple-element.66), channel_id=1, source_target_pairs={{0,4},{2,6},{4,0},{6,2},{1,5},{3,7},{5,1},{7,3},{8,12},{10,14},{12... | collective-permute-start | bytes 589832 | tf_op jit(solution)/shard_map/ppermute | solution.py:52
  75.2 14.6 %collective-permute-start.9 = (bf16[96,1024]{1,0:T(8,128)(2,1)S(1)}, bf16[96,1024]{1,0:T(8,128)(2,1)S(1)}, u32[]{:S(2)}, u32[]{:S(2)}) collective-permute-start(bf16[96,1024]{1,0:T(8,128)(2,1)S(1)} %get-tuple-element.50.refs_4_), channel_id=1, source_target_pairs={{0,16},{8,24},{16,0},{24,8},{1,17},{9,25},{17,1},{25,9},{2,18},{10... | collective-permute-start | bytes 589832 | tf_op jit(solution)/shard_map/ppermute | solution.py:26
  107.3 17.2 %collective-permute-start.11 = (bf16[96,4096]{1,0:T(8,128)(2,1)S(1)}, bf16[96,4096]{1,0:T(8,128)(2,1)S(1)}, u32[]{:S(2)}, u32[]{:S(2)}) collective-permute-start(bf16[96,4096]{1,0:T(8,128)(2,1)S(1)} %all_gather.6.refs_0_), channel_id=1, source_target_pairs={{0,8},{8,0},{16,24},{24,16},{1,9},{9,1},{17,25},{25,17},{2,10},{10... | collective-permute-start | bytes 2359304 | tf_op jit(solution)/shard_map/ppermute | solution.py:33
  107.3 17.2 %collective-permute-start.12 = (bf16[96,4096]{1,0:T(8,128)(2,1)S(1)}, bf16[96,4096]{1,0:T(8,128)(2,1)S(1)}, u32[]{:S(2)}, u32[]{:S(2)}) collective-permute-start(bf16[96,4096]{1,0:T(8,128)(2,1)S(1)} %collective-permute-done.4.refs_1_), channel_id=1, source_target_pairs={{0,8},{8,0},{16,24},{24,16},{1,9},{9,1},{17,25},{25,17},{2,10},{10... | collective-permute-start | bytes 2359304 | tf_op jit(solution)/shard_map/ppermute | solution.py:33
  110.6 23.1 %collective-permute-start.10 = (bf16[96,4096]{1,0:T(8,128)(2,1)S(1)}, bf16[96,4096]{1,0:T(8,128)(2,1)S(1)}, u32[]{:S(2)}, u32[]{:S(2)}) collective-permute-start(bf16[96,4096]{1,0:T(8,128)(2,1)S(1)} %all_gather.7.refs_4_), channel_id=1, source_target_pairs={{0,16},{8,24},{16,0},{24,8},{1,17},{9,25},{17,1},{25,9},{2,18},{10... | collective-permute-start | bytes 2359304 | tf_op jit(solution)/shard_map/ppermute | solution.py:26
  112.2 4.4 %collective-permute-start.19 = (f32[24]{0:T(128)S(1)}, f32[24]{0:T(128)S(1)}, u32[]{:S(2)}, u32[]{:S(2)}) collective-permute-start(f32[24]{0:T(128)S(1)} %get-tuple-element.74), channel_id=1, source_target_pairs={{0,4},{2,6},{4,0},{6,2},{1,5},{3,7},{5,1},{7,3},{8,12},{10,14},{12... | collective-permute-start | bytes 296 | tf_op jit(solution)/shard_map/ppermute | solution.py:52
  113.0 3.6 %collective-permute-start.20 = (f32[24]{0:T(128)S(1)}, f32[24]{0:T(128)S(1)}, u32[]{:S(2)}, u32[]{:S(2)}) collective-permute-start(f32[24]{0:T(128)S(1)} %get-tuple-element.75), channel_id=1, source_target_pairs={{0,6},{2,0},{4,2},{6,4},{1,7},{3,1},{5,3},{7,5},{8,14},{10,8},{12,... | collective-permute-start | bytes 296 | tf_op jit(solution)/shard_map/ppermute | solution.py:52
  116.7 5.3 %collective-permute-start.18 = (f32[24]{0:T(128)S(1)}, f32[24]{0:T(128)S(1)}, u32[]{:S(2)}, u32[]{:S(2)}) collective-permute-start(f32[24]{0:T(128)S(1)} %get-tuple-element.76), channel_id=1, source_target_pairs={{0,2},{2,4},{4,6},{6,0},{1,3},{3,5},{5,7},{7,1},{8,10},{10,12},{12... | collective-permute-start | bytes 296 | tf_op jit(solution)/shard_map/ppermute | solution.py:52
  116.7 5.9 %collective-permute-start.17 = (bf16[96,1024]{1,0:T(8,128)(2,1)S(1)}, bf16[96,1024]{1,0:T(8,128)(2,1)S(1)}, u32[]{:S(2)}, u32[]{:S(2)}) collective-permute-start(bf16[96,1024]{1,0:T(8,128)(2,1)S(1)} %convolution_convert_fusion.2), channel_id=1, source_target_pairs={{0,1},{1,0},{2,3},{3,2},{4,5},{5,4},{6,7},{7,6},{8,9},{9,8},{10,11... | collective-permute-start | bytes 589832 | tf_op jit(solution)/shard_map/ppermute | solution.py:42
  122.0 1.8 %collective-permute-start.13 = (bf16[96,1024]{1,0:T(8,128)(2,1)S(1)}, bf16[96,1024]{1,0:T(8,128)(2,1)S(1)}, u32[]{:S(2)}, u32[]{:S(2)}) collective-permute-start(bf16[96,1024]{1,0:T(8,128)(2,1)S(1)} %get-tuple-element.50.refs_4_), channel_id=1, source_target_pairs={{0,8},{8,0},{16,24},{24,16},{1,9},{9,1},{17,25},{25,17},{2,10},{10... | collective-permute-start | bytes 589832 | tf_op jit(solution)/shard_map/ppermute | solution.py:33
  122.6 1.6 %collective-permute-start.14 = (bf16[96,1024]{1,0:T(8,128)(2,1)S(1)}, bf16[96,1024]{1,0:T(8,128)(2,1)S(1)}, u32[]{:S(2)}, u32[]{:S(2)}) collective-permute-start(bf16[96,1024]{1,0:T(8,128)(2,1)S(1)} %collective-permute-done.9.refs_5_), channel_id=1, source_target_pairs={{0,8},{8,0},{16,24},{24,16},{1,9},{9,1},{17,25},{25,17},{2,10},{10... | collective-permute-start | bytes 589832 | tf_op jit(solution)/shard_map/ppermute | solution.py:33
  123.8 9.9 %collective-permute-start.15 = (bf16[96,1024]{1,0:T(8,128)(2,1)S(1)}, bf16[96,1024]{1,0:T(8,128)(2,1)S(1)}, u32[]{:S(2)}, u32[]{:S(2)}) collective-permute-start(bf16[96,1024]{1,0:T(8,128)(2,1)S(1)} %copy-done), channel_id=1, source_target_pairs={{0,8},{8,0},{16,24},{24,16},{1,9},{9,1},{17,25},{25,17},{2,10},{10... | collective-permute-start | bytes 589832 | tf_op jit(solution)/shard_map/ppermute | solution.py:33
  124.2 9.5 %collective-permute-start.16 = (bf16[96,1024]{1,0:T(8,128)(2,1)S(1)}, bf16[96,1024]{1,0:T(8,128)(2,1)S(1)}, u32[]{:S(2)}, u32[]{:S(2)}) collective-permute-start(bf16[96,1024]{1,0:T(8,128)(2,1)S(1)} %collective-permute-done.5.refs_1_), channel_id=1, source_target_pairs={{0,8},{8,0},{16,24},{24,16},{1,9},{9,1},{17,25},{25,17},{2,10},{10... | collective-permute-start | bytes 589832 | tf_op jit(solution)/shard_map/ppermute | solution.py:33
  133.7 2.4 %collective-permute-start.21 = (bf16[96,4096]{1,0:T(8,128)(2,1)S(1)}, bf16[96,4096]{1,0:T(8,128)(2,1)S(1)}, u32[]{:S(2)}, u32[]{:S(2)}) collective-permute-start(bf16[96,4096]{1,0:T(8,128)(2,1)S(1)} %all_gather.7.refs_4_), channel_id=1, source_target_pairs={{0,8},{8,0},{16,24},{24,16},{1,9},{9,1},{17,25},{25,17},{2,10},{10... | collective-permute-start | bytes 2359304 | tf_op jit(solution)/shard_map/ppermute | solution.py:33
  133.9 3.3 %collective-permute-start.22 = (bf16[96,4096]{1,0:T(8,128)(2,1)S(1)}, bf16[96,4096]{1,0:T(8,128)(2,1)S(1)}, u32[]{:S(2)}, u32[]{:S(2)}) collective-permute-start(bf16[96,4096]{1,0:T(8,128)(2,1)S(1)} %collective-permute-done.10.refs_5_), channel_id=1, source_target_pairs={{0,8},{8,0},{16,24},{24,16},{1,9},{9,1},{17,25},{25,17},{2,10},{10... | collective-permute-start | bytes 2359304 | tf_op jit(solution)/shard_map/ppermute | solution.py:33
